TPU v7x, 128 devices: a whole 4x4x4 slice. The times are simulated.
128 devices in a mesh: rep: 32 (over z_hi, y, x), shard: 4 (over z_lo, core).
Axes of the slice: x: 4, y: 4, z: 4 (z_hi: 2, z_lo: 2; z = z_hi * 2 + z_lo), core: 2. Of those that a mesh axis runs over, the one named last changes fastest.
Arguments:
- hidden: bfloat16 [16384, 1024], P(('rep', 'shard')), may hold values from -6 to 6
- cotangent: bfloat16 [16384, 1024], P(('rep', 'shard')), may hold values from -6 to 6
- segment_ids: int32 [16384], P('rep'), may hold values from 0 to 2, as said below
- positions: int32 [16384], P('rep'), may hold values from 0 to 2560, as said below
- attention_gain: float32 [1024], P('shard'), may hold values from 0.1 to 1.9
- query_weight: float32 [1024, 2048], P('shard'), may hold values from -0.1875 to 0.1875
- key_weight: float32 [1024, 1024], P('shard'), may hold values from -0.1875 to 0.1875
- value_weight: float32 [1024, 1024], P('shard'), may hold values from -0.1875 to 0.1875
- query_gain: float32 [128], P('shard'), may hold values from 0.1 to 1.9
- key_gain: float32 [128], P('shard'), may hold values from 0.1 to 1.9
- headgate_weight: float32 [1024, 16], P('shard'), may hold values from -0.1875 to 0.1875
- headgate_bias: float32 [16], P('shard'), may hold values from -3 to 3
- output_weight: float32 [2048, 1024], P('shard'), may hold values from -3.5 to 3.5
- feedforward_gain: float32 [1024], P('shard'), may hold values from 0.1 to 1.9
- gate_weight: float32 [1024, 3072], P('shard'), may hold values from -0.1875 to 0.1875
- up_weight: float32 [1024, 3072], P('shard'), may hold values from -0.1875 to 0.1875
- down_weight: float32 [3072, 1024], P('shard'), may hold values from -0.109375 to 0.109375
Outputs:
- output: bfloat16 [16384, 1024], P(('rep', 'shard'))
- input_grad: bfloat16 [16384, 1024], P(('rep', 'shard'))
- grad_attention_gain: float32 [1024], P('shard')
- grad_query_weight: float32 [1024, 2048], P('shard')
- grad_key_weight: float32 [1024, 1024], P('shard')
- grad_value_weight: float32 [1024, 1024], P('shard')
- grad_query_gain: float32 [128], P('shard')
- grad_key_gain: float32 [128], P('shard')
- grad_headgate_weight: float32 [1024, 16], P('shard')
- grad_headgate_bias: float32 [16], P('shard')
- grad_output_weight: float32 [2048, 1024], P('shard')
- grad_feedforward_gain: float32 [1024], P('shard')
- grad_gate_weight: float32 [1024, 3072], P('shard')
- grad_up_weight: float32 [1024, 3072], P('shard')
- grad_down_weight: float32 [3072, 1024], P('shard')
Inputs may be any that keep to these rules, and one draw needn't show every extreme that they name: `segment_ids`: within each sequence of 512 tokens the document numbers start at 0 and never fall. `positions`: positions rise by one from token to token within a document; each sequence's first token has position 0 and its last token position 2560.
All inputs are finite; a program needn't handle non-finite values.
Results may differ from a plain program's by a relative error of at most 0.029.
Values may be sent and summed in bfloat16 or wider, within the bound.
No kernel may reach another device: no remote copies, remote signals or barrier semaphores. Data moves between devices by JAX's collectives and lax.ppermute only.
A program may use at most 192 MiB of HBM per device.

v0:
```python
import math

import jax
import jax.numpy as jnp
from jax import lax
from jax.sharding import PartitionSpec as P

epsilon = 1e-06
theta = 1000000.0
masked_score = -1e30


def tables(places, head_size):
    half = head_size // 2
    freq = jnp.power(jnp.float32(theta), -jnp.arange(half, dtype=jnp.float32) * 2.0 / head_size)
    angle = places.astype(jnp.float32)[:, None] * freq[None, :]
    return (jnp.cos(angle), jnp.sin(angle))


def rotate(value, cosine, sine):
    half = value.shape[-1] // 2
    first = value[..., :half]
    second = value[..., half:]
    cosine = cosine[:, None, :]
    sine = sine[:, None, :]
    return jnp.concatenate([first * cosine - second * sine, second * cosine + first * sine], -1)


def rotate_back(grad, cosine, sine):
    half = grad.shape[-1] // 2
    first = grad[..., :half]
    second = grad[..., half:]
    cosine = cosine[:, None, :]
    sine = sine[:, None, :]
    return jnp.concatenate([first * cosine + second * sine, second * cosine - first * sine], -1)


def inverse_rms(value):
    return lax.rsqrt(jnp.mean(value * value, -1, keepdims=True) + epsilon)


def norm_back(grad, normal, inverse):
    return inverse * (grad - normal * jnp.mean(grad * normal, -1, keepdims=True))


def weight_grad(left, right):
    return jnp.einsum("la,lb->ab", left, right, preferred_element_type=jnp.float32)


def back_product(grad, weight):
    return jnp.einsum("lb,ab->la", grad, weight, preferred_element_type=jnp.float32)


def head_norm_rope(raw, gain, cosine, sine):
    inverse = inverse_rms(raw)
    normal = raw * inverse
    return (
        normal,
        inverse,
        rotate(normal * gain.astype(jnp.float32), cosine, sine).astype(jnp.bfloat16),
    )


def head_norm_back(grad, normal, inverse, gain, cosine, sine):
    turned = rotate_back(grad, cosine, sine)
    gain_grad = jnp.sum(turned * normal, (0, 1))
    raw_grad = norm_back(turned * gain.astype(jnp.float32), normal, inverse).astype(jnp.bfloat16)
    return (gain_grad, raw_grad)


def split_heads(query_low, keys_low, values_low):
    count, heads, head_size = query_low.shape
    kv_heads = keys_low.shape[1]
    query_heads = query_low.reshape(count, kv_heads, heads // kv_heads, head_size).transpose(
        1, 2, 0, 3
    )
    return (query_heads, keys_low.transpose(1, 0, 2), values_low.transpose(1, 0, 2))


def attention_forward(query_low, keys_low, values_low, allowed, scale):
    count, heads, head_size = query_low.shape
    query_heads, keys_heads, values_heads = split_heads(query_low, keys_low, values_low)

    def forward_head(items):
        query_part, keys_part, values_part = items
        scores = (
            jnp.einsum("glh,sh->gls", query_part, keys_part, preferred_element_type=jnp.float32)
            * scale
        )
        scores = jnp.where(allowed[None], scores, masked_score)
        peak = jnp.max(scores, -1, keepdims=True)
        expo = jnp.exp(scores - peak)
        total = jnp.sum(expo, -1, keepdims=True)
        probs = expo / total
        result = jnp.einsum(
            "gls,sh->glh",
            probs.astype(jnp.bfloat16),
            values_part,
            preferred_element_type=jnp.float32,
        )
        return (result, peak[..., 0] + jnp.log(total[..., 0]))

    attended, logsum = lax.map(forward_head, (query_heads, keys_heads, values_heads))
    return (attended.transpose(2, 0, 1, 3).reshape(count, heads, head_size), logsum)


def attention_backward(query_low, keys_low, values_low, allowed, scale, logsum, grad_attended):
    count, heads, head_size = query_low.shape
    kv_heads = keys_low.shape[1]
    query_heads, keys_heads, values_heads = split_heads(query_low, keys_low, values_low)
    grad_heads = grad_attended.reshape(count, kv_heads, heads // kv_heads, head_size).transpose(
        1, 2, 0, 3
    )

    def backward_head(items):
        query_part, keys_part, values_part, grad_part, logsum_part = items
        scores = (
            jnp.einsum("glh,sh->gls", query_part, keys_part, preferred_element_type=jnp.float32)
            * scale
        )
        scores = jnp.where(allowed[None], scores, masked_score)
        probs = jnp.exp(scores - logsum_part[..., None])
        grad_probs = jnp.einsum(
            "glh,sh->gls", grad_part, values_part, preferred_element_type=jnp.float32
        )
        grad_values = jnp.einsum(
            "gls,glh->sh", probs.astype(jnp.bfloat16), grad_part, preferred_element_type=jnp.float32
        )
        grad_scores = probs * (grad_probs - jnp.sum(probs * grad_probs, -1, keepdims=True))
        grad_scores = grad_scores.astype(jnp.bfloat16)
        grad_query = (
            jnp.einsum("gls,sh->glh", grad_scores, keys_part, preferred_element_type=jnp.float32)
            * scale
        )
        grad_keys = (
            jnp.einsum("gls,glh->sh", grad_scores, query_part, preferred_element_type=jnp.float32)
            * scale
        )
        return (grad_query, grad_keys, grad_values)

    query_terms, key_terms, value_terms = lax.map(
        backward_head, (query_heads, keys_heads, values_heads, grad_heads, logsum)
    )
    grad_query = query_terms.transpose(2, 0, 1, 3).reshape(count, heads, head_size)
    return (grad_query, key_terms.transpose(1, 0, 2), value_terms.transpose(1, 0, 2))


def body(
    hidden,
    cotangent,
    segment_ids,
    positions,
    attention_gain,
    query_weight,
    key_weight,
    value_weight,
    query_gain,
    key_gain,
    headgate_weight,
    headgate_bias,
    output_weight,
    feedforward_gain,
    gate_weight,
    up_weight,
    down_weight,
):
    half_type = jnp.bfloat16
    full_type = jnp.float32
    local_rows = hidden.shape[0]
    shards = lax.axis_size("shard")
    shard_index = lax.axis_index("shard")
    first_row = shard_index * local_rows
    inputs = hidden.astype(full_type)
    upstream = cotangent.astype(full_type)
    fetched = (
        lax.all_gather(attention_gain.astype(half_type), "shard", axis=0, tiled=True),
        lax.all_gather(query_weight.astype(half_type), "shard", axis=0, tiled=True),
        lax.all_gather(key_weight.astype(half_type), "shard", axis=0, tiled=True),
        lax.all_gather(value_weight.astype(half_type), "shard", axis=0, tiled=True),
        lax.all_gather(query_gain.astype(half_type), "shard", axis=0, tiled=True),
        lax.all_gather(key_gain.astype(half_type), "shard", axis=0, tiled=True),
        lax.all_gather(headgate_weight.astype(half_type), "shard", axis=0, tiled=True),
        lax.all_gather(headgate_bias.astype(half_type), "shard", axis=0, tiled=True),
        lax.all_gather(output_weight.astype(half_type), "shard", axis=0, tiled=True),
        lax.all_gather(feedforward_gain.astype(half_type), "shard", axis=0, tiled=True),
        lax.all_gather(gate_weight.astype(half_type), "shard", axis=0, tiled=True),
        lax.all_gather(up_weight.astype(half_type), "shard", axis=0, tiled=True),
        lax.all_gather(down_weight.astype(half_type), "shard", axis=0, tiled=True),
    )
    (
        gain_first,
        query_full,
        keys_full,
        values_full,
        qgain_full,
        kgain_full,
        headgate_full,
        headbias_full,
        output_full,
        gain_second,
        gate_full,
        upward_full,
        down_full,
    ) = fetched
    heads = headgate_full.shape[1]
    head_size = qgain_full.shape[0]
    kv_heads = keys_full.shape[1] // head_size
    length = local_rows * shards
    scale = 1.0 / math.sqrt(head_size)
    inv_first = inverse_rms(inputs)
    normed_first = inputs * inv_first
    attn_in = (normed_first * gain_first.astype(full_type)).astype(half_type)
    query_raw = jnp.dot(attn_in, query_full, preferred_element_type=full_type).reshape(
        local_rows, heads, head_size
    )
    keys_raw = jnp.dot(attn_in, keys_full, preferred_element_type=full_type).reshape(
        local_rows, kv_heads, head_size
    )
    values_low = jnp.dot(attn_in, values_full, preferred_element_type=full_type).astype(half_type)
    values_low = values_low.reshape(local_rows, kv_heads, head_size)
    gate_logit = jnp.dot(
        attn_in, headgate_full, preferred_element_type=full_type
    ) + headbias_full.astype(full_type)
    local_positions = lax.dynamic_slice_in_dim(positions, first_row, local_rows)
    cosine, sine = tables(local_positions, head_size)
    query_normed, inv_query, query_low = head_norm_rope(query_raw, qgain_full, cosine, sine)
    keys_normed, inv_keys, keys_low = head_norm_rope(keys_raw, kgain_full, cosine, sine)
    all_keys, all_values = (
        lax.all_gather(keys_low, "shard", axis=0, tiled=True),
        lax.all_gather(values_low, "shard", axis=0, tiled=True),
    )
    local_segments = lax.dynamic_slice_in_dim(segment_ids, first_row, local_rows)
    query_places = first_row + jnp.arange(local_rows)
    allowed = (jnp.arange(length)[None, :] <= query_places[:, None]) & (
        local_segments[:, None] == segment_ids[None, :]
    )
    attended, logsum = attention_forward(query_low, all_keys, all_values, allowed, scale)
    gate_value = jax.nn.sigmoid(gate_logit)
    mixed_low = (
        (attended * gate_value[:, :, None]).astype(half_type).reshape(local_rows, heads * head_size)
    )
    resid = inputs + jnp.dot(mixed_low, output_full, preferred_element_type=full_type)
    inv_second = inverse_rms(resid)
    normed_second = resid * inv_second
    ffn_in = (normed_second * gain_second.astype(full_type)).astype(half_type)
    gate_pre = jnp.dot(ffn_in, gate_full, preferred_element_type=full_type)
    up_pre = jnp.dot(ffn_in, upward_full, preferred_element_type=full_type)
    sigma = jax.nn.sigmoid(gate_pre)
    swish = gate_pre * sigma
    act_low = (swish * up_pre).astype(half_type)
    output = (resid + jnp.dot(act_low, down_full, preferred_element_type=full_type)).astype(
        half_type
    )
    grad_down = weight_grad(act_low, cotangent)
    grad_act = back_product(cotangent, down_full)
    grad_gate_pre = (grad_act * up_pre * sigma * (1.0 + gate_pre * (1.0 - sigma))).astype(half_type)
    grad_up_pre = (grad_act * swish).astype(half_type)
    grad_gate_w = weight_grad(ffn_in, grad_gate_pre)
    grad_up_w = weight_grad(ffn_in, grad_up_pre)
    grad_ffn_in = back_product(grad_gate_pre, gate_full) + back_product(grad_up_pre, upward_full)
    grad_gain_second = jnp.sum(grad_ffn_in * normed_second, 0)
    grad_resid = upstream + norm_back(
        grad_ffn_in * gain_second.astype(full_type), normed_second, inv_second
    )
    resid_low = grad_resid.astype(half_type)
    grad_output_w = weight_grad(mixed_low, resid_low)
    grad_mixed = back_product(resid_low, output_full).reshape(local_rows, heads, head_size)
    grad_gate_value = jnp.sum(grad_mixed * attended, -1)
    grad_logit_low = (grad_gate_value * gate_value * (1.0 - gate_value)).astype(half_type)
    grad_headbias = jnp.sum(grad_logit_low.astype(full_type), 0)
    grad_headgate = weight_grad(attn_in, grad_logit_low)
    grad_attended = (grad_mixed * gate_value[:, :, None]).astype(half_type)
    grad_query, key_terms, value_terms = attention_backward(
        query_low, all_keys, all_values, allowed, scale, logsum, grad_attended
    )
    grad_keys, grad_values = (
        lax.psum_scatter(
            key_terms.astype(jnp.bfloat16), "shard", scatter_dimension=0, tiled=True
        ).astype(jnp.float32),
        lax.psum_scatter(
            value_terms.astype(jnp.bfloat16), "shard", scatter_dimension=0, tiled=True
        ).astype(jnp.float32),
    )
    grad_qgain, grad_query_raw = head_norm_back(
        grad_query, query_normed, inv_query, qgain_full, cosine, sine
    )
    grad_kgain, grad_keys_raw = head_norm_back(
        grad_keys, keys_normed, inv_keys, kgain_full, cosine, sine
    )
    grad_query_raw = grad_query_raw.reshape(local_rows, heads * head_size)
    grad_keys_raw = grad_keys_raw.reshape(local_rows, kv_heads * head_size)
    grad_values_low = grad_values.astype(half_type).reshape(local_rows, kv_heads * head_size)
    grad_query_w = weight_grad(attn_in, grad_query_raw)
    grad_key_w = weight_grad(attn_in, grad_keys_raw)
    grad_value_w = weight_grad(attn_in, grad_values_low)
    grad_attn_in = (
        back_product(grad_query_raw, query_full)
        + back_product(grad_keys_raw, keys_full)
        + back_product(grad_values_low, values_full)
        + back_product(grad_logit_low, headgate_full)
    )
    grad_gain_first = jnp.sum(grad_attn_in * normed_first, 0)
    grad_inputs = grad_resid + norm_back(
        grad_attn_in * gain_first.astype(full_type), normed_first, inv_first
    )
    input_grad = grad_inputs.astype(half_type)
    owned = (
        lax.psum_scatter(
            grad_gain_first.astype(jnp.bfloat16), "shard", scatter_dimension=0, tiled=True
        ).astype(jnp.float32),
        lax.psum_scatter(
            grad_query_w.astype(jnp.bfloat16), "shard", scatter_dimension=0, tiled=True
        ).astype(jnp.float32),
        lax.psum_scatter(
            grad_key_w.astype(jnp.bfloat16), "shard", scatter_dimension=0, tiled=True
        ).astype(jnp.float32),
        lax.psum_scatter(
            grad_value_w.astype(jnp.bfloat16), "shard", scatter_dimension=0, tiled=True
        ).astype(jnp.float32),
        lax.psum_scatter(
            grad_qgain.astype(jnp.bfloat16), "shard", scatter_dimension=0, tiled=True
        ).astype(jnp.float32),
        lax.psum_scatter(
            grad_kgain.astype(jnp.bfloat16), "shard", scatter_dimension=0, tiled=True
        ).astype(jnp.float32),
        lax.psum_scatter(
            grad_headgate.astype(jnp.bfloat16), "shard", scatter_dimension=0, tiled=True
        ).astype(jnp.float32),
        lax.psum_scatter(
            grad_headbias.astype(jnp.bfloat16), "shard", scatter_dimension=0, tiled=True
        ).astype(jnp.float32),
        lax.psum_scatter(
            grad_output_w.astype(jnp.bfloat16), "shard", scatter_dimension=0, tiled=True
        ).astype(jnp.float32),
        lax.psum_scatter(
            grad_gain_second.astype(jnp.bfloat16), "shard", scatter_dimension=0, tiled=True
        ).astype(jnp.float32),
        lax.psum_scatter(
            grad_gate_w.astype(jnp.bfloat16), "shard", scatter_dimension=0, tiled=True
        ).astype(jnp.float32),
        lax.psum_scatter(
            grad_up_w.astype(jnp.bfloat16), "shard", scatter_dimension=0, tiled=True
        ).astype(jnp.float32),
        lax.psum_scatter(
            grad_down.astype(jnp.bfloat16), "shard", scatter_dimension=0, tiled=True
        ).astype(jnp.float32),
    )
    summed = (
        lax.psum(owned[0].astype(jnp.bfloat16), "rep").astype(jnp.float32),
        lax.psum(owned[1].astype(jnp.bfloat16), "rep").astype(jnp.float32),
        lax.psum(owned[2].astype(jnp.bfloat16), "rep").astype(jnp.float32),
        lax.psum(owned[3].astype(jnp.bfloat16), "rep").astype(jnp.float32),
        lax.psum(owned[4].astype(jnp.bfloat16), "rep").astype(jnp.float32),
        lax.psum(owned[5].astype(jnp.bfloat16), "rep").astype(jnp.float32),
        lax.psum(owned[6].astype(jnp.bfloat16), "rep").astype(jnp.float32),
        lax.psum(owned[7].astype(jnp.bfloat16), "rep").astype(jnp.float32),
        lax.psum(owned[8].astype(jnp.bfloat16), "rep").astype(jnp.float32),
        lax.psum(owned[9].astype(jnp.bfloat16), "rep").astype(jnp.float32),
        lax.psum(owned[10].astype(jnp.bfloat16), "rep").astype(jnp.float32),
        lax.psum(owned[11].astype(jnp.bfloat16), "rep").astype(jnp.float32),
        lax.psum(owned[12].astype(jnp.bfloat16), "rep").astype(jnp.float32),
    )
    return (
        output,
        input_grad,
        summed[0],
        summed[1],
        summed[2],
        summed[3],
        summed[4],
        summed[5],
        summed[6],
        summed[7],
        summed[8],
        summed[9],
        summed[10],
        summed[11],
        summed[12],
    )


def solution(mesh):
    return jax.shard_map(
        body,
        mesh=mesh,
        in_specs=(
            P(("rep", "shard"), None),
            P(("rep", "shard"), None),
            P("rep"),
            P("rep"),
            P("shard"),
            P("shard", None),
            P("shard", None),
            P("shard", None),
            P("shard"),
            P("shard"),
            P("shard", None),
            P("shard"),
            P("shard", None),
            P("shard"),
            P("shard", None),
            P("shard", None),
            P("shard", None),
        ),
        out_specs=(
            P(("rep", "shard"), None),
            P(("rep", "shard"), None),
            P("shard"),
            P("shard", None),
            P("shard", None),
            P("shard", None),
            P("shard"),
            P("shard"),
            P("shard", None),
            P("shard"),
            P("shard", None),
            P("shard"),
            P("shard", None),
            P("shard", None),
            P("shard", None),
        ),
        check_vma=False,
    )
```

profile of v0, /device:TPU:0, one launch (start us, length us, event | category | flops | bytes accessed | tf_op | source)
XLA Modules:
  0.0 1354.8 jit_solution(14936494011847533552)
XLA Ops:
  13.1 5.1 all-gather
  20.8 8.0 all-reduce.11
  30.1 11.8 all-gather.14.cloned.1.call-done
  46.2 28.1 %all-gather.18.cloned.1.call-done = bf16[1024,1024]{1,0:T(8,128)(2,1)} async-done(((bf16[256,1024]{1,0:T(8,128)(2,1)}), bf16[1024,1024]{1,0:T(8,128)(2,1)}) %all-gather.18.cloned.1.call-update) | async-done | bytes 2097168 | tf_op jit(solution)/shard_map/all_gather | solution.py:179
  77.2 2.7 convert_element_type.262
  80.0 3.3 convert_element_type.266
  83.3 3.3 convert_element_type.267
  86.7 3.6 convert_element_type.269
  90.5 5.3 all_gather.53
  95.9 5.1 all-gather.1
  101.2 22.7 %all-gather.12.cloned.1.call-done = bf16[1024,2048]{1,0:T(8,128)(2,1)} async-done(((bf16[256,2048]{1,0:T(8,128)(2,1)}), bf16[1024,2048]{1,0:T(8,128)(2,1)}) %all-gather.12.cloned.1.call-update) | async-done | bytes 4194320 | tf_op jit(solution)/shard_map/all_gather | solution.py:177
  123.9 3.0 fusion.95
  130.1 18.0 %all-gather.16.cloned.1.call-done = bf16[512,8,128]{2,0,1:T(8,128)(2,1)} async-done(((bf16[128,8,128]{2,0,1:T(8,128)(2,1)}), bf16[512,8,128]{2,0,1:T(8,128)(2,1)}) %all-gather.16.cloned.1.call-update) | async-done | bytes 1048592 | tf_op jit(solution)/shard_map/all_gather | solution.py:229
  148.1 23.8 %all-gather.20.cloned.1.call-done = bf16[512,8,128]{2,0,1:T(8,128)(2,1)} async-done(((bf16[128,8,128]{2,0,1:T(8,128)(2,1)}), bf16[512,8,128]{2,0,1:T(8,128)(2,1)}) %all-gather.20.cloned.1.call-update) | async-done | bytes 1048592 | tf_op jit(solution)/shard_map/all_gather | solution.py:230
  172.1 27.7 %while.28 = (s32[]{:T(128)}, f32[8,2,128,128]{3,2,1,0:T(8,128)S(1)}, f32[8,2,128]{2,1,0:T(2,128)}, bf16[8,2,128,128]{3,2,1,0:T(8,128)(2,1)}, bf16[8,512,128]{2,1...) while((s32[]{:T(128)}, ...), condition=%wide.region_6.7_spmd.clone, body=%wide.region_3.6_spmd.clone.sunk | while | flops 68353792 | bytes 2176613 | solution.py:103
  203.2 17.9 %all-gather.22.cloned.1.call-done = bf16[2048,1024]{1,0:T(8,128)(2,1)} async-done(((bf16[512,1024]{1,0:T(8,128)(2,1)}), bf16[2048,1024]{1,0:T(8,128)(2,1)}) %all-gather.22.cloned.1.call-update) | async-done | bytes 4194320 | tf_op jit(solution)/shard_map/all_gather | solution.py:184
  221.1 3.2 multiply_reduce_fusion.6
  224.5 63.5 %all-gather.24.cloned.1.call-done = bf16[1024,3072]{1,0:T(8,128)(2,1)} async-done(((bf16[256,3072]{1,0:T(8,128)(2,1)}), bf16[1024,3072]{1,0:T(8,128)(2,1)}) %all-gather.24.cloned.1.call-update) | async-done | bytes 6291472 | tf_op jit(solution)/shard_map/all_gather | solution.py:186
  288.0 4.9 fusion.101
  292.9 62.3 %all-gather.26.cloned.1.call-done = bf16[1024,3072]{1,0:T(8,128)(2,1)} async-done(((bf16[256,3072]{1,0:T(8,128)(2,1)}), bf16[1024,3072]{1,0:T(8,128)(2,1)}) %all-gather.26.cloned.1.call-update) | async-done | bytes 6291472 | tf_op jit(solution)/shard_map/all_gather | solution.py:187
  355.2 4.9 fusion.102
  360.1 62.3 %all-gather.28.cloned.1.call-done = bf16[3072,1024]{1,0:T(8,128)(2,1)} async-done(((bf16[768,1024]{1,0:T(8,128)(2,1)}), bf16[3072,1024]{1,0:T(8,128)(2,1)}) %all-gather.28.cloned.1.call-update) | async-done | bytes 6291472 | tf_op jit(solution)/shard_map/all_gather | solution.py:188
  422.3 7.0 multiply_convert_fusion.1
  429.4 5.6 fusion.103
  435.0 2.8 multiply_reduce_fusion.3
  441.2 3.1 reshape.223
  447.9 70.0 %while.29 = (s32[]{:T(128)}, f32[8,2,128,128]{3,2,1,0:T(8,128)}, bf16[8,512,128]{2,1,0:T(8,128)(2,1)}, bf16[8,512,128]{1,2,0:T(8,128)(2,1)}, bf16[8,2,128,128]{3...) while((s32[]{:T(128)}, f32[8,2,128,128]{3,2,1,0:T(8,128)}, ...), condition=%wide.region_11.12_spmd.clone, body=%wide.region_9.11_spmd.clone.sunk | while | flops 169246464 | bytes 5387393 | solution.py:141
  521.0 19.0 %reduce-scatter.13.cloned.1.call-done = bf16[128,8,128]{2,0,1:T(8,128)(2,1)} async-done(((bf16[512,8,128]{2,0,1:T(8,128)(2,1)}), bf16[128,8,128]{2,0,1:T(8,128)(2,1)}) %reduce-scatter.13.cloned.1.call-update) | async-done | bytes 262160 | tf_op jit(solution)/shard_map/reduce_scatter | solution.py:277
  544.9 2.8 convolution_convert_fusion.6
  547.7 16.8 %reduce-scatter.31.cloned.1.call-done = bf16[128,1024]{1,0:T(8,128)(2,1)} async-done(((bf16[512,1024]{1,0:T(8,128)(2,1)}), bf16[128,1024]{1,0:T(8,128)(2,1)}) %reduce-scatter.31.cloned.1.call-update) | async-done | bytes 262160 | tf_op jit(solution)/shard_map/reshape | solution.py:292
  564.5 3.1 convolution_convert_fusion.5
  575.0 3.3 convolution_convert_fusion.4
  579.4 3.3 convolution_convert_fusion.3
  583.8 4.5 convolution_convert_fusion.2
  589.4 4.4 convolution_convert_fusion.1
  595.1 4.5 convolution_convert_fusion
  603.0 26.1 %reduce-scatter.19.cloned.1.call-done = bf16[256,1024]{1,0:T(8,128)(2,1)} async-done(((bf16[1024,1024]{1,0:T(8,128)(2,1)}), bf16[256,1024]{1,0:T(8,128)(2,1)}) %reduce-scatter.19.cloned.1.call-update) | async-done | bytes 524304 | tf_op jit(solution)/shard_map/reduce_scatter | solution.py:317
  629.1 48.7 %reduce-scatter.15.cloned.1.call-done = bf16[256,2048]{1,0:T(8,128)(2,1)} async-done(((bf16[1024,2048]{1,0:T(8,128)(2,1)}), bf16[256,2048]{1,0:T(8,128)(2,1)}) %reduce-scatter.15.cloned.1.call-update) | async-done | bytes 1048592 | tf_op jit(solution)/shard_map/reduce_scatter | solution.py:311
  677.8 48.8 %reduce-scatter.23.cloned.1.call-done = bf16[512,1024]{1,0:T(8,128)(2,1)} async-done(((bf16[2048,1024]{1,0:T(8,128)(2,1)}), bf16[512,1024]{1,0:T(8,128)(2,1)}) %reduce-scatter.23.cloned.1.call-update) | async-done | bytes 1048592 | tf_op jit(solution)/shard_map/reduce_scatter | solution.py:332
  726.6 65.8 %reduce-scatter.25.cloned.1.call-done = bf16[256,3072]{1,0:T(8,128)(2,1)} async-done(((bf16[1024,3072]{1,0:T(8,128)(2,1)}), bf16[256,3072]{1,0:T(8,128)(2,1)}) %reduce-scatter.25.cloned.1.call-update) | async-done | bytes 1572880 | tf_op jit(solution)/shard_map/reduce_scatter | solution.py:338
  792.4 65.8 %reduce-scatter.27.cloned.1.call-done = bf16[256,3072]{1,0:T(8,128)(2,1)} async-done(((bf16[1024,3072]{1,0:T(8,128)(2,1)}), bf16[256,3072]{1,0:T(8,128)(2,1)}) %reduce-scatter.27.cloned.1.call-update) | async-done | bytes 1572880 | tf_op jit(solution)/shard_map/reduce_scatter | solution.py:341
  858.2 65.8 %reduce-scatter.29.cloned.1.call-done = bf16[768,1024]{1,0:T(8,128)(2,1)} async-done(((bf16[3072,1024]{1,0:T(8,128)(2,1)}), bf16[768,1024]{1,0:T(8,128)(2,1)}) %reduce-scatter.29.cloned.1.call-update) | async-done | bytes 1572880 | tf_op jit(solution)/shard_map/reduce_scatter | solution.py:344
  926.0 4.6 fusion.52
  934.9 5.9 all-reduce.10
  941.2 3.5 reduce-scatter.21.cloned.1.call-done
  944.7 183.5 %all-reduce.8 = (bf16[256]{0:T(256)(128)(2,1)S(1)}, bf16[32]{0:T(256)(128)(2,1)S(1)}, bf16[32]{0:T(256)(128)(2,1)S(1)}, bf16[256,16]{0,1:T(8,128)(2,1)S(1)}, bf1...) all-reduce(bf16[256]{0:T(256)(128)(2,1)S(1)} %dynamic-slice.4, ...), channel_id=1, replica_groups=mesh['rep'=32,'shard'=4] {'rep'}, use_global_device_ids=true, to_apply=%region_20.21 | all-reduce | flops 4676 | bytes 18704 | tf_op jit(solution)/shard_map/psum | solution.py:349
  1132.3 202.2 %all-reduce.14.cloned.1.call-done = (bf16[256,2048]{1,0:T(8,128)(2,1)}, bf16[256,1024]{1,0:T(8,128)(2,1)}, bf16[256,1024]{1,0:T(8,128)(2,1)}, bf16[512,1024]{1,0...) async-done(((bf16[256,2048]{1,0:T(8,128)(2,1)}, bf16[256,1024]{1,0:T(8,128)(2,1)}, bf16[256,1024]{1,0:T(8,128)(2,1)}, ...) | async-done | bytes 7864336 | tf_op jit(solution)/shard_map/psum | solution.py:350
  1334.6 3.6 convert_element_type.305
  (370 shorter events, 168.1 us)
Async XLA Ops:
  7.2 4.6 copy-start.18
  7.2 34.7 %all-gather.14.cloned.1.call-start = ((), (), s32[]{:S(2)}) async-start(), calls=%async_computation.11 | async-start | bytes 2621440 | tf_op jit(solution)/shard_map/all_gather | solution.py:178
  9.5 8.6 copy-start.54
  9.5 8.6 copy-start.55
  9.5 8.7 copy-start.51
  9.5 10.5 copy-start.56
  9.6 20.1 %copy-start.1 = (bf16[128,1024]{1,0:T(8,128)(2,1)S(1)}, bf16[128,1024]{1,0:T(8,128)(2,1)}, u32[]{:S(2)}) copy-start(bf16[128,1024]{1,0:T(8,128)(2,1)} %param.21) | copy-start | bytes 786436
  9.6 64.7 %all-gather.18.cloned.1.call-start = ((), (), s32[]{:S(2)}) async-start(), calls=%async_computation.13 | async-start | bytes 2621440 | tf_op jit(solution)/shard_map/all_gather | solution.py:179
  11.8 112.1 %all-gather.12.cloned.1.call-start = ((), (), s32[]{:S(2)}) async-start(), calls=%async_computation.10 | async-start | bytes 5242880 | tf_op jit(solution)/shard_map/all_gather | solution.py:177
  13.0 135.2 %all-gather.16.cloned.1.call-start = ((), (), s32[]{:S(2)}) async-start(), calls=%async_computation.12 | async-start | bytes 1310720 | tf_op jit(solution)/shard_map/all_gather | solution.py:229
  28.8 16.4 %copy-start.46 = (f32[128]{0:T(128)}, f32[128]{0:T(128)S(1)}, u32[]{:S(2)}) copy-start(f32[128]{0:T(128)S(1)} %convert_element_type.255) | copy-start | bytes 1540
  29.8 94.1 %copy-start.41 = (f32[128]{0:T(128)}, f32[128]{0:T(128)S(1)}, u32[]{:S(2)}) copy-start(f32[128]{0:T(128)S(1)} %add_rsqrt_fusion.3) | copy-start | bytes 1540
  46.2 125.8 %all-gather.20.cloned.1.call-start = ((), (), s32[]{:S(2)}) async-start(), calls=%async_computation.14 | async-start | bytes 1310720 | tf_op jit(solution)/shard_map/all_gather | solution.py:230
  77.1 144.0 %all-gather.22.cloned.1.call-start = ((), (), s32[]{:S(2)}) async-start(), calls=%async_computation.15 | async-start | bytes 5242880 | tf_op jit(solution)/shard_map/all_gather | solution.py:184
  79.9 208.0 %all-gather.24.cloned.1.call-start = ((), (), s32[]{:S(2)}) async-start(), calls=%async_computation.16 | async-start | bytes 7864320 | tf_op jit(solution)/shard_map/all_gather | solution.py:186
  83.3 271.9 %all-gather.26.cloned.1.call-start = ((), (), s32[]{:S(2)}) async-start(), calls=%async_computation.17 | async-start | bytes 7864320 | tf_op jit(solution)/shard_map/all_gather | solution.py:187
  86.6 9.2 copy-start.53
  86.6 335.7 %all-gather.28.cloned.1.call-start = ((), (), s32[]{:S(2)}) async-start(), calls=%async_computation.18 | async-start | bytes 7864320 | tf_op jit(solution)/shard_map/all_gather | solution.py:188
  90.3 449.7 %reduce-scatter.13.cloned.1.call-start = ((), (), s32[]{:S(2)}) async-start(), calls=%async_computation.19 | async-start | bytes 1310720 | tf_op jit(solution)/shard_map/reduce_scatter | solution.py:277
  90.4 37.4 %copy-start.48 = (f32[128]{0:T(128)}, f32[128]{0:T(128)S(1)}, u32[]{:S(2)}) copy-start(f32[128]{0:T(128)S(1)} %convert_element_type.251) | copy-start | bytes 1540
  95.9 31.2 %copy-start.31 = (bf16[1024,16]{0,1:T(8,128)(2,1)}, bf16[1024,16]{0,1:T(8,128)(2,1)S(1)}, u32[]{:S(2)}) copy-start(bf16[1024,16]{0,1:T(8,128)(2,1)S(1)} %all_gather.53) | copy-start | bytes 98308
  100.9 123.4 %copy-start.33 = (f32[4,1,256]{2,1,0:T(1,128)}, f32[4,1,256]{2,1,0:T(1,128)S(1)}, u32[]{:S(2)}) copy-start(f32[4,1,256]{2,1,0:T(1,128)S(1)} %convert_element_type.311) | copy-start | bytes 12292
  199.8 24.5 %copy-start.37 = (s32[128]{0:T(128)}, s32[128]{0:T(128)S(1)}, u32[]{:S(2)}) copy-start(s32[128]{0:T(128)S(1)} %get-tuple-element.578) | copy-start | bytes 1540
  199.8 24.5 %copy-start.39 = (s32[128]{0:T(128)}, s32[128]{0:T(128)S(1)}, u32[]{:S(2)}) copy-start(s32[128]{0:T(128)S(1)} %get-tuple-element.579) | copy-start | bytes 1540
  224.3 210.6 %copy-start.50 = (f32[128]{0:T(128)}, f32[128]{0:T(128)S(1)}, u32[]{:S(2)}) copy-start(f32[128]{0:T(128)S(1)} %add_rsqrt_fusion.2) | copy-start | bytes 1540
  292.9 129.5 %copy-start.25 = (bf16[128,1024]{1,0:T(8,128)(2,1)S(1)}, bf16[128,1024]{1,0:T(8,128)(2,1)}, u32[]{:S(2)}) copy-start(bf16[128,1024]{1,0:T(8,128)(2,1)} %param.22) | copy-start | bytes 786436
  429.4 5.6 copy-start.16
  429.4 5.6 copy-start.14
  429.4 5.6 copy-start
  429.4 5.6 copy-start.34
  441.2 6.6 copy-start.38
  441.2 6.6 copy-start.40
  517.9 46.6 %reduce-scatter.31.cloned.1.call-start = ((), (), s32[]{:S(2)}) async-start(), calls=%async_computation.28 | async-start | bytes 1310720 | tf_op jit(solution)/shard_map/reshape | solution.py:292
  520.3 82.7 %reduce-scatter.17.cloned.1.call-start = ((), (), s32[]{:S(2)}) async-start(), calls=%async_computation.21 | async-start | bytes 2621440 | tf_op jit(solution)/shard_map/reduce_scatter | solution.py:314
  542.9 21.6 %copy-start.42 = (f32[128]{0:T(128)S(1)}, f32[128]{0:T(128)}, u32[]{:S(2)}) copy-start(f32[128]{0:T(128)} %copy-done.41) | copy-start | bytes 1540
  547.6 20.0 %copy-start.49 = (f32[128]{0:T(128)S(1)}, f32[128]{0:T(128)}, u32[]{:S(2)}) copy-start(f32[128]{0:T(128)} %copy-done.48) | copy-start | bytes 1540
  547.7 81.5 %reduce-scatter.19.cloned.1.call-start = ((), (), s32[]{:S(2)}) async-start(), calls=%async_computation.22 | async-start | bytes 2621440 | tf_op jit(solution)/shard_map/reduce_scatter | solution.py:317
  567.6 110.2 %reduce-scatter.15.cloned.1.call-start = ((), (), s32[]{:S(2)}) async-start(), calls=%async_computation.20 | async-start | bytes 5242880 | tf_op jit(solution)/shard_map/reduce_scatter | solution.py:311
  578.4 148.3 %reduce-scatter.23.cloned.1.call-start = ((), (), s32[]{:S(2)}) async-start(), calls=%async_computation.24 | async-start | bytes 5242880 | tf_op jit(solution)/shard_map/reduce_scatter | solution.py:332
  582.7 209.7 %reduce-scatter.25.cloned.1.call-start = ((), (), s32[]{:S(2)}) async-start(), calls=%async_computation.25 | async-start | bytes 7864320 | tf_op jit(solution)/shard_map/reduce_scatter | solution.py:338
  588.3 269.9 %reduce-scatter.27.cloned.1.call-start = ((), (), s32[]{:S(2)}) async-start(), calls=%async_computation.26 | async-start | bytes 7864320 | tf_op jit(solution)/shard_map/reduce_scatter | solution.py:341
  593.9 330.1 %reduce-scatter.29.cloned.1.call-start = ((), (), s32[]{:S(2)}) async-start(), calls=%async_computation.27 | async-start | bytes 7864320 | tf_op jit(solution)/shard_map/reduce_scatter | solution.py:344
  599.6 345.1 %reduce-scatter.21.cloned.1.call-start = ((), (), s32[]{:S(2)}) async-start(), calls=%async_computation.23 | async-start | bytes 40960 | tf_op jit(solution)/shard_map/reduce_scatter | solution.py:326
  602.9 731.6 %all-reduce.14.cloned.1.call-start = ((), (), s32[]{:S(2)}) async-start(), calls=%async_computation.29 | async-start | bytes 15728640 | tf_op jit(solution)/shard_map/psum | solution.py:350
  926.0 4.7 copy-start.43
  926.0 4.7 copy-start.8
  926.0 5.5 copy-start.9
  926.0 5.5 copy-start.27
  (29 other events, 62.5 us)
Sparse Core Ops, SparseCore 0:
  10.3 31.6 all-gather.13
  44.2 30.0 all-gather.17
  76.5 47.3 all-gather.11
  126.0 22.1 all-gather.15
  150.2 21.6 all-gather.19
  174.1 47.0 all-gather.21
  223.4 64.5 all-gather.23
  290.2 64.8 all-gather.25
  357.4 64.8 all-gather.27
  518.0 21.8 reduce-scatter.12
  543.1 21.3 reduce-scatter.30
  567.4 29.3 reduce-scatter.16
  599.8 29.2 reduce-scatter.18
  631.4 46.3 reduce-scatter.14
  680.2 46.3 reduce-scatter.22
  728.9 63.4 reduce-scatter.24
  794.7 63.4 reduce-scatter.26
  860.5 63.4 reduce-scatter.28
  926.9 17.6 reduce-scatter.20
  947.9 386.6 all-reduce.13
where the time goes:
time: 1360 us; the launch traced here: 1350 us
  waiting for transfers between devices  873 us (64%)
  blocking collectives  213 us (16%)
  matrix products  155 us (11%)
  other arithmetic  64.6 us (5%)
  local copies, waits for them, and re-layouts  28.2 us (2%)
  between operations  18.8 us (1%)
    psum x1, waiting for transfers between devices, body(): lax.psum(owned[1].astype(jnp.bfloat16), 'rep').astype(jnp.float32)  202 us
    psum x1, blocking collectives, body(): lax.psum(owned[0].astype(jnp.bfloat16), 'rep').astype(jnp.float32)  183 us
    reduce_scatter x1, waiting for transfers between devices, body(): lax.psum_scatter(grad_down.astype(jnp.bfloat16), 'shard', scatter_dimensi...  65.8 us
    reduce_scatter x1, waiting for transfers between devices, body(): lax.psum_scatter(grad_gate_w.astype(jnp.bfloat16), 'shard', scatter_dimen...  65.8 us
    reduce_scatter x1, waiting for transfers between devices, body(): lax.psum_scatter(grad_up_w.astype(jnp.bfloat16), 'shard', scatter_dimensi...  65.8 us
    all_gather x1, waiting for transfers between devices, body(): lax.all_gather(gate_weight.astype(half_type), 'shard', axis=0, tiled=True)  63.5 us
    all_gather x1, waiting for transfers between devices, body(): lax.all_gather(down_weight.astype(half_type), 'shard', axis=0, tiled=True)  62.3 us
    all_gather x1, waiting for transfers between devices, body(): lax.all_gather(up_weight.astype(half_type), 'shard', axis=0, tiled=True)  62.3 us
  transfers between devices with their start and end apart: 20, of which 19 were waited for; matrix products, arithmetic and copies ran while one was open for 10% of the time, Pallas kernels for 0%

commit v1 on v0

v1 whole, which is shorter than its diff:
```python
import functools
import math

import jax
import jax.numpy as jnp
from jax import lax
from jax.experimental import pallas as pl
from jax.experimental.pallas import tpu as pltpu
from jax.sharding import Mesh
from jax.sharding import PartitionSpec as P

EPS = 1e-06
THETA = 1000000.0
MASKED = -1e30
HEAD = 128
LOW = jnp.bfloat16
FULL = jnp.float32
AXES = ("zh", "y", "x", "zl", "core")
GROUP = ("zl", "core")
LANES = 128
STREAMS = (
    (("x", 1), ("x", 3), ("y", 1), ("y", 3)),
    (("x", 3), ("x", 1), ("y", 3), ("y", 1)),
    (("y", 1), ("y", 3), ("x", 1), ("x", 3)),
    (("y", 3), ("y", 1), ("x", 3), ("x", 1)),
)
SIZE = {"zh": 2, "y": 4, "x": 4, "zl": 2, "core": 2}
DEST = (0, 2, 1, 3)


def swap(value, axis, mask):
    return lax.ppermute(value, axis, [(i, i ^ mask) for i in range(SIZE[axis])])


def turn(value, step):
    return lax.ppermute(value, ("zh", "zl"), [(i, (i + step) % 4) for i in range(4)])


def place_block(stream, pos, mine_x, mine_y):
    rel = {"x": 0, "y": 0}
    for k, (axis, mask) in enumerate(STREAMS[stream]):
        bit = (pos >> (3 - k)) & 1
        rel[axis] = rel[axis] ^ (mask * bit)
    return (mine_y ^ rel["y"]) * 4 + (mine_x ^ rel["x"])


def dot(left, right):
    return jnp.dot(left, right, preferred_element_type=FULL)


def dot_t(left, right):
    return lax.dot_general(left, right, (((1,), (1,)), ((), ())), preferred_element_type=FULL)


def dot_tn(left, right):
    return lax.dot_general(left, right, (((0,), (0,)), ((), ())), preferred_element_type=FULL)


def spread_kernel(coords, left_c, right_c, left_r, right_r, *refs):
    outs, (held_c, held_r) = refs[:8], refs[8:]
    mine_x, mine_y, j = coords[0], coords[1], coords[2]
    panels = right_c.shape[1] // (4 * LANES)
    wide = panels * LANES
    rows_r = left_r.shape[1] // 16
    base = 4 * panels * 16
    for s in range(4):
        keep, send = outs[s], outs[4 + s]
        held_c[...] = dot_tn(left_c[...], right_c[:, s * wide : (s + 1) * wide]).astype(LOW)
        held_r[...] = dot_tn(left_r[...], right_r[:, s * 256 : (s + 1) * 256]).astype(LOW)

        for pos in range(16):
            block = place_block(s, pos, mine_x, mine_y)
            out, at = (keep, pos) if pos < 8 else (send, pos - 8)
            for d in range(4):
                row = pl.multiple_of((j ^ DEST[d]) * 256 + block * 16, 16)
                for p in range(panels):
                    low = (d * panels + p) * 16
                    out[at, low : low + 16, :] = held_c[pl.ds(row, 16), p * LANES : (p + 1) * LANES]
            row = pl.multiple_of(block * rows_r, 16)
            for p in range(2):
                low = base + p * rows_r
                out[at, low : low + rows_r, :] = held_r[pl.ds(row, rows_r), p * LANES : (p + 1) * LANES]


def spread(coords, left_c, right_c, left_r, right_r):
    panels = right_c.shape[1] // 512
    rows = 4 * panels * 16 + 2 * (left_r.shape[1] // 16)
    vmem = pl.BlockSpec(memory_space=pltpu.VMEM)
    return pl.pallas_call(
        spread_kernel,
        out_shape=[jax.ShapeDtypeStruct((8, rows, LANES), LOW)] * 8,
        in_specs=[pl.BlockSpec(memory_space=pltpu.SMEM)] + [vmem] * 4,
        out_specs=[vmem] * 8,
        scratch_shapes=[
            pltpu.VMEM((left_c.shape[1], panels * LANES), LOW),
            pltpu.VMEM((left_r.shape[1], 256), LOW),
        ],
        compiler_params=pltpu.CompilerParams(vmem_limit_bytes=48 * 2**20),
        cost_estimate=pl.CostEstimate(
            flops=2 * 512 * (left_c.shape[1] * right_c.shape[1] + left_r.shape[1] * right_r.shape[1]),
            bytes_accessed=2 * 16 * 4 * rows * LANES,
            transcendentals=0,
        ),
    )(coords, left_c, right_c, left_r, right_r)


def settle_kernel(widths, coords, *refs):
    ins, outs = refs[:8], refs[8:]
    mine_x, mine_y, j = coords[0], coords[1], coords[2]
    panels = sum(widths) // 512
    rows_r = outs[-1].shape[0] // 16
    base = 4 * panels * 16
    spots = []
    for t in range(4 * panels):
        col, w = t * LANES, 0
        while col >= widths[w]:
            col, w = col - widths[w], w + 1
        spots.append((w, col))

    for s in range(4):
        for pos in range(16):
            block = place_block(s, pos, mine_x, mine_y)
            got, at = (ins[s], pos) if pos < 8 else (ins[4 + s], pos - 8)
            row = pl.multiple_of(block * 16, 16)
            for r in range(4):
                for p in range(panels):
                    w, col = spots[s * panels + p]
                    lane = pl.multiple_of((j ^ r) * widths[w] + col, LANES)
                    low = (r * panels + p) * 16
                    outs[w][pl.ds(row, 16), pl.ds(lane, LANES)] = got[at, low : low + 16, :].astype(FULL)
            row = pl.multiple_of(block * rows_r, 16)
            for p in range(2):
                low = base + p * rows_r
                lane = s * 256 + p * LANES
                outs[-1][pl.ds(row, rows_r), lane : lane + LANES] = got[at, low : low + rows_r, :].astype(FULL)


def settle(coords, pieces, widths, rows_r):
    vmem = pl.BlockSpec(memory_space=pltpu.VMEM)
    shapes = [(256, 4 * w) for w in widths] + [(rows_r, 1024)]
    return pl.pallas_call(
        functools.partial(settle_kernel, widths),
        out_shape=[jax.ShapeDtypeStruct(s, FULL) for s in shapes],
        in_specs=[pl.BlockSpec(memory_space=pltpu.SMEM)] + [vmem] * 8,
        out_specs=[vmem] * len(shapes),
        compiler_params=pltpu.CompilerParams(vmem_limit_bytes=48 * 2**20),
        cost_estimate=pl.CostEstimate(
            flops=0, bytes_accessed=6 * sum(a * b for a, b in shapes), transcendentals=0
        ),
    )(coords, *pieces)


def sum_over_replicas(pieces, panels):
    kept, sent = list(pieces[:4]), list(pieces[4:])
    for k in range(4):
        got = [swap(sent[s], *STREAMS[s][k]) for s in range(4)]
        both = [kept[s] + got[s] for s in range(4)]
        if k < 3:
            half = 4 >> k
            kept, sent = [b[:half] for b in both], [b[half:] for b in both]
    whole = jnp.concatenate(both, 0)
    base = 4 * panels * 16
    columns = whole[:, :base].reshape(4, 4, panels * 16, LANES)
    rows = whole[:, base:]
    got = swap(columns[:, 2:], "core", 1)
    mine = jnp.stack([columns[:, 0], got[:, 0]], 1).reshape(4, base // 2, LANES)
    other = jnp.stack([columns[:, 1], got[:, 1]], 1).reshape(4, base // 2, LANES)
    mine = jnp.concatenate([mine, rows], 1)
    mine = mine + swap(mine, "zh", 1)
    other = turn(other, 1) + turn(other, -1)
    whole = jnp.concatenate([mine[:, : base // 2], other, mine[:, base // 2 :]], 1)
    held = [whole[s : s + 1] for s in range(4)]
    for k in (3, 2, 1):
        got = [swap(held[s], *STREAMS[s][k]) for s in range(4)]
        held = [jnp.concatenate([held[s], got[s]], 0) for s in range(4)]
    return held + [swap(held[s], *STREAMS[s][0]) for s in range(4)]


def group_gather(part):
    beside = swap(part, "core", 1)
    across = swap(part, "zl", 1)
    return jnp.stack([part, beside, across, swap(across, "core", 1)])


def group_scatter(parts):
    got = swap(jnp.stack([parts[1], parts[3]]).astype(LOW), "core", 1).astype(FULL)
    mine, other = parts[0] + got[0], parts[2] + got[1]
    return mine + swap(other.astype(LOW), "zl", 1).astype(FULL)


def take_columns(weights, widths, j):
    blocks = [
        jnp.concatenate(
            [lax.dynamic_slice_in_dim(w, (j ^ r) * n, n, 1) for w, n in zip(weights, widths)], 1
        ).astype(LOW)
        for r in range(4)
    ]
    got = swap(jnp.stack([blocks[1], blocks[3]]), "core", 1)
    ahead, behind = turn(blocks[2], 1), turn(got[1], -1)
    rel = jnp.stack([blocks[0], got[0], ahead, behind])
    return jnp.concatenate(
        [lax.dynamic_index_in_dim(rel, j ^ r, 0, False) for r in range(4)], 0
    )


def inverse_rms(value):
    return lax.rsqrt(jnp.mean(value * value, -1, keepdims=True) + EPS)


def norm_back(grad, normal, inverse):
    return inverse * (grad - normal * jnp.mean(grad * normal, -1, keepdims=True))


def rotate(value, cosine, sine):
    first, second = value[..., :64], value[..., 64:]
    return jnp.concatenate([first * cosine - second * sine, second * cosine + first * sine], -1)


def body(
    hidden,
    cotangent,
    segment_ids,
    positions,
    attention_gain,
    query_weight,
    key_weight,
    value_weight,
    query_gain,
    key_gain,
    headgate_weight,
    headgate_bias,
    output_weight,
    feedforward_gain,
    gate_weight,
    up_weight,
    down_weight,
):
    zl, core = lax.axis_index("zl"), lax.axis_index("core")
    j = zl * 2 + core
    coords = jnp.stack([lax.axis_index("x"), lax.axis_index("y"), j]).astype(jnp.int32)
    order = j ^ jnp.arange(4)

    small = jnp.concatenate(
        [
            attention_gain,
            feedforward_gain,
            query_gain,
            key_gain,
            headgate_bias,
            headgate_weight.reshape(-1),
            jnp.zeros(5120 - 4676, FULL),
        ]
    ).astype(LOW)
    small = lax.all_gather(small.reshape(40, 128), GROUP, axis=0, tiled=True).reshape(4, 5120).astype(FULL)
    gain_first = small[:, :256].reshape(1024)
    gain_second = small[:, 256:512].reshape(1024)
    gain_query = small[:, 512:544].reshape(128)
    gain_key = small[:, 544:576].reshape(128)
    head_bias = lax.dynamic_slice_in_dim(small[:, 576:580].reshape(16), 4 * j, 4)
    head_weight = lax.dynamic_slice_in_dim(small[:, 580:4676].reshape(1024, 16), 4 * j, 4, 1).astype(LOW)

    tokens = group_gather(hidden).reshape(512, 1024)
    weight_qkv = take_columns((query_weight, key_weight, value_weight), (512, 256, 256), j)
    grads = group_gather(cotangent).reshape(512, 1024)
    weight_gu = take_columns((gate_weight, up_weight), (768, 768), j)
    weight_o = output_weight.astype(LOW)
    weight_d = down_weight.astype(LOW)

    segs = jnp.take(segment_ids.reshape(4, 128), order, axis=0).reshape(512)
    spots = jnp.take(positions.reshape(4, 128), order, axis=0).reshape(512)
    index = (order[:, None] * 128 + jnp.arange(128)[None, :]).reshape(512)
    allowed = (index[None, :] <= index[:, None]) & (segs[:, None] == segs[None, :])
    freq = jnp.power(jnp.float32(THETA), -jnp.arange(64, dtype=FULL) * 2.0 / HEAD)
    angle = spots.astype(FULL)[:, None] * freq[None, :]
    cosine, sine = jnp.cos(angle)[:, None, :], jnp.sin(angle)[:, None, :]
    scale = 1.0 / math.sqrt(HEAD)

    x = tokens.astype(FULL)
    inv_first = inverse_rms(x)
    normed_first = x * inv_first
    attn_in = (normed_first * gain_first).astype(LOW)
    raw = dot(attn_in, weight_qkv)
    query_raw = raw[:, :512].reshape(512, 4, HEAD)
    key_raw = raw[:, 512:768].reshape(512, 2, HEAD)
    value = raw[:, 768:].astype(LOW).reshape(512, 2, HEAD)
    logit = dot(attn_in, head_weight) + head_bias
    inv_q, inv_k = inverse_rms(query_raw), inverse_rms(key_raw)
    norm_q, norm_k = query_raw * inv_q, key_raw * inv_k
    query = rotate(norm_q * gain_query, cosine, sine).astype(LOW)
    key = rotate(norm_k * gain_key, cosine, sine).astype(LOW)
    q4 = query.reshape(512, 2, 2, HEAD)
    scores = jnp.einsum("lkgh,skh->kgls", q4, key, preferred_element_type=FULL) * scale
    scores = jnp.where(allowed, scores, MASKED)
    expo = jnp.exp(scores - jnp.max(scores, -1, keepdims=True))
    probs = expo / jnp.sum(expo, -1, keepdims=True)
    probs_low = probs.astype(LOW)
    attended = jnp.einsum("kgls,skh->lkgh", probs_low, value, preferred_element_type=FULL).reshape(512, 4, HEAD)
    gate = jax.nn.sigmoid(logit)
    mixed = (attended * gate[:, :, None]).astype(LOW).reshape(512, 512)
    resid = hidden.astype(FULL) + group_scatter(dot(mixed, weight_o).reshape(4, 128, 1024))

    inv_second = inverse_rms(resid)
    normed_second = resid * inv_second
    ffn_in = group_gather((normed_second * gain_second).astype(LOW)).reshape(512, 1024)
    gu = dot(ffn_in, weight_gu)
    gate_pre, up_pre = gu[:, :768], gu[:, 768:]
    sigma = jax.nn.sigmoid(gate_pre)
    swish = gate_pre * sigma
    act = (swish * up_pre).astype(LOW)
    grad_act = dot_t(grads, weight_d)
    grad_gate = (grad_act * up_pre * sigma * (1.0 + gate_pre * (1.0 - sigma))).astype(LOW)
    grad_up = (grad_act * swish).astype(LOW)
    grad_gu = jnp.concatenate([grad_gate, grad_up], 1)
    grad_ffn = group_scatter(dot_t(grad_gu, weight_gu).reshape(4, 128, 1024))
    output = (resid + group_scatter(dot(act, weight_d).reshape(4, 128, 1024))).astype(LOW)
    first = sum_over_replicas(spread(coords, ffn_in, grad_gu, act, grads), 3)
    grad_g, grad_u, grad_d = settle(coords, first, (768, 768), 768)

    grad_gain_second = jnp.sum(grad_ffn * normed_second, 0)
    grad_resid = cotangent.astype(FULL) + norm_back(grad_ffn * gain_second, normed_second, inv_second)
    resid_low = group_gather(grad_resid.astype(LOW)).reshape(512, 1024)

    grad_mixed = dot_t(resid_low, weight_o).reshape(512, 4, HEAD)
    grad_logit = (jnp.sum(grad_mixed * attended, -1) * gate * (1.0 - gate)).astype(LOW)
    grad_attended = (grad_mixed * gate[:, :, None]).astype(LOW).reshape(512, 2, 2, HEAD)
    grad_probs = jnp.einsum("lkgh,skh->kgls", grad_attended, value, preferred_element_type=FULL)
    grad_value = jnp.einsum("kgls,lkgh->skh", probs_low, grad_attended, preferred_element_type=FULL)
    grad_scores = (probs * (grad_probs - jnp.sum(probs * grad_probs, -1, keepdims=True))).astype(LOW)
    grad_query = jnp.einsum("kgls,skh->lkgh", grad_scores, key, preferred_element_type=FULL) * scale
    grad_key = jnp.einsum("kgls,lkgh->skh", grad_scores, q4, preferred_element_type=FULL) * scale

    def head_back(grad, normal, inverse, gain):
        turned = rotate(grad, cosine, -sine)
        return jnp.sum(turned * normal, (0, 1)), norm_back(turned * gain, normal, inverse).astype(LOW)

    grad_qgain, grad_q = head_back(grad_query.reshape(512, 4, HEAD), norm_q, inv_q, gain_query)
    grad_kgain, grad_k = head_back(grad_key, norm_k, inv_k, gain_key)
    grad_qkv = jnp.concatenate(
        [grad_q.reshape(512, 512), grad_k.reshape(512, 256), grad_value.astype(LOW).reshape(512, 256)], 1
    )
    grad_in = dot_t(grad_qkv, weight_qkv) + dot_t(grad_logit, head_weight)
    second = sum_over_replicas(spread(coords, attn_in, grad_qkv, mixed, resid_low), 2)
    grad_qw, grad_kw, grad_vw, grad_ow = settle(coords, second, (512, 256, 256), 512)
    grad_headgate = dot_tn(attn_in, grad_logit)
    grad_headbias = jnp.sum(grad_logit.astype(FULL), 0)
    grad_gain_first = jnp.sum(grad_in * normed_first, 0)
    mine = group_scatter(grad_in.reshape(4, 128, 1024))
    own = hidden.astype(FULL)
    inv_own = inverse_rms(own)
    input_grad = (grad_resid + norm_back(mine * gain_first, own * inv_own, inv_own)).astype(LOW)

    small = jnp.concatenate(
        [grad_gain_first, grad_gain_second, grad_qgain, grad_kgain, grad_headgate.reshape(-1), grad_headbias]
    )
    small = jnp.pad(small, (0, 6528 - small.shape[0])).reshape(51, 128)
    for axis, mask in STREAMS[0] + (("zh", 1),):
        small = small + swap(small, axis, mask)
    gains = small[:18]
    heads = lax.dynamic_update_slice_in_dim(jnp.zeros((4, 33, 128), FULL), small[None, 18:], j, 0).reshape(132, 128)
    small = jnp.concatenate([gains, heads])
    for axis in GROUP:
        small = small + swap(small, axis, 1)
    heads = small[18:].reshape(4, 33 * 128)
    heads_w = heads[:, :4096].reshape(4, 1024, 4).transpose(1, 0, 2).reshape(-1)
    small = jnp.concatenate([small[:18].reshape(-1), heads_w, heads[:, 4096:4100].reshape(-1)])

    def quarter(start, size):
        return lax.dynamic_slice_in_dim(small, start + j * size, size)

    return (
        output,
        input_grad,
        quarter(0, 256),
        grad_qw,
        grad_kw,
        grad_vw,
        quarter(2048, 32),
        quarter(2176, 32),
        quarter(2304, 4096).reshape(256, 16),
        quarter(2304 + 16384, 4),
        grad_ow,
        quarter(1024, 256),
        grad_g,
        grad_u,
        grad_d,
    )


def solution(mesh):
    grid = Mesh(mesh.devices.reshape(2, 4, 4, 2, 2), AXES)
    tokens, split, copies = P(AXES, None), P(GROUP, None), P(("zh", "y", "x"))
    line = P(GROUP)
    return jax.shard_map(
        body,
        mesh=grid,
        in_specs=(
            tokens,
            tokens,
            copies,
            copies,
            line,
            split,
            split,
            split,
            line,
            line,
            split,
            line,
            split,
            line,
            split,
            split,
            split,
        ),
        out_specs=(
            tokens,
            tokens,
            line,
            split,
            split,
            split,
            line,
            line,
            split,
            line,
            split,
            line,
            split,
            split,
            split,
        ),
        check_vma=False,
    )
```

time: 1360 us -> 455 us (0.33)
  waiting for transfers between devices: 873 us -> 144 us
  blocking collectives: 213 us -> 7.87 us
  matrix products: 155 us -> 31.3 us
  starting transfers between devices: 1.09 us -> 110 us
  local copies, waits for them, and re-layouts: 28.2 us -> 65.7 us
  Pallas kernels: 0 us -> 19.2 us
  between operations: 18.8 us -> 3.51 us
    reduce_scatter x9 -> x0, waiting for transfers between devices: 343 us -> none  [the longest x1 65.8 us: body(): lax.psum_scatter(grad_down.astype(jnp.bfloat16), 'shard', scatter_dimensi...]
    all_gather x9 -> x0, waiting for transfers between devices: 310 us -> none  [the longest x1 63.5 us: body(): lax.all_gather(gate_weight.astype(half_type), 'shard', axis=0, tiled=True)]
    psum x1 -> x0, waiting for transfers between devices: 202 us -> none  [body(): lax.psum(owned[1].astype(jnp.bfloat16), 'rep').astype(jnp.float32)]
    psum x1 -> x0, blocking collectives: 183 us -> none  [body(): lax.psum(owned[0].astype(jnp.bfloat16), 'rep').astype(jnp.float32)]
    ppermute x0 -> x105, waiting for transfers between devices: none -> 144 us  [the longest x97 117 us: swap(): return lax.ppermute(value, axis, [(i, i ^ mask) for i in range(SIZE[axis])])]
    dot_general x80 -> x16, matrix products: 155 us -> 26.1 us  [the longest x5 8.89 us: dot_t(): lax.dot_general(left, right, (((1,), (1,)), ((), ())), preferred_element_...]
    ppermute x0 -> x105, starting transfers between devices: none -> 110 us  [the longest x97 96.6 us: swap(): return lax.ppermute(value, axis, [(i, i ^ mask) for i in range(SIZE[axis])])]
    convert_element_type x44 -> x16, other arithmetic: 40.4 us -> 15.3 us  [the longest x4 3.53 us: group_scatter(): swap(jnp.stack([parts[1], parts[3]]).astype(LOW), 'core', 1).astype(FULL)]
  transfers between devices with their start and end apart: 20 -> 105, of which waited for: 19 -> 47; matrix products, arithmetic and copies ran while one was open for 10% -> 33% of each run, Pallas kernels for 0% -> 3%
where the time goes in v1:
time: 455 us; the launch traced here: 447 us
  waiting for transfers between devices  144 us (32%)
  starting transfers between devices  110 us (24%)
  local copies, waits for them, and re-layouts  65.7 us (14%)
  other arithmetic  65.3 us (14%)
  matrix products  31.3 us (7%)
  Pallas kernels  19.2 us (4%)
  blocking collectives  7.87 us (2%)
    ppermute x97, waiting for transfers between devices, swap(): return lax.ppermute(value, axis, [(i, i ^ mask) for i in range(SIZE[axis])])  117 us
    ppermute x97, starting transfers between devices, swap(): return lax.ppermute(value, axis, [(i, i ^ mask) for i in range(SIZE[axis])])  96.6 us
    ppermute x8, waiting for transfers between devices, turn(): lax.ppermute(value, ('zh', 'zl'), [(i, (i + step) % 4) for i in range(4)])  27.5 us
    unnamed x248, local copies, waits for them, and re-layouts  16.3 us
    ppermute x8, starting transfers between devices, turn(): lax.ppermute(value, ('zh', 'zl'), [(i, (i + step) % 4) for i in range(4)])  13.8 us
    concatenate x24, other arithmetic, sum_over_replicas(): held = [jnp.concatenate([held[s], got[s]], 0) for s in range(4)]  10.8 us
    pallas_call x2, Pallas kernels, spread(): pl.pallas_call(spread_kernel, out_shape=[jax.ShapeDtypeStruct((8, rows, L...  9.84 us
    pallas_call x2, Pallas kernels, settle(): pl.pallas_call(functools.partial(settle_kernel, widths), out_shape=[jax.S...  9.33 us
  transfers between devices with their start and end apart: 105, of which 47 were waited for; matrix products, arithmetic and copies ran while one was open for 33% of the time, Pallas kernels for 3%

profile of v1, /device:TPU:0, one launch (start us, length us, event | category | flops | bytes accessed | tf_op | source)
XLA Modules:
  0.0 447.5 jit_solution(7724333158502335116)
XLA Ops:
  8.1 7.9 %all_gather.3 = bf16[160,128]{1,0:T(8,128)(2,1)S(1)} all-gather(bf16[40,128]{1,0:T(8,128)(2,1)S(1)} %bitcast.418), channel_id=1, replica_groups=mesh['zh'=2,'y'=4,'x'=4,'zl'=2,'core'=2] {'zl','core'}, dimensions={0}, use_global_device_ids=true | all-gather | bytes 51200 | tf_op jit(solution)/shard_map/all_gather | solution.py:254
  19.0 4.0 fusion.64
  30.0 2.8 convert_element_type.212
  37.9 2.4 collective-permute-start.5
  42.5 7.7 %collective-permute-done.4 = bf16[256,1024]{1,0:T(8,128)(2,1)} collective-permute-done((bf16[256,1024]{1,0:T(8,128)(2,1)}, bf16[256,1024]{1,0:T(8,128)(2,1)}, u32[]{:S(2)}, u32[]{:S(2)}) %collective-permute-start.4) | collective-permute-done | bytes 524320 | tf_op jit(solution)/shard_map/ppermute | solution.py:36
  66.7 5.2 %fusion.131 = (f32[2,2,512]{2,1,0:T(2,128)S(1)}, f32[2,2,512,512]{2,3,1,0:T(8,128)}) fusion(pred[512,512]{0,1:T(8,128)(4,1)} %compare_and_fusion, bf16[512,2,64]{2,0,1:T(8,128)(2,1)} %get-tuple-element.200, bf16[512,2,64]{2,0,1:T(8,128)(2,1)} %get-tuple-element.199, bf16[512,2,2,64]{3,0,2,1:T(8,128)(2,1)S(1)} %bitcast.373, ...), kind=kOutput, calls=%fused_computation.351 | convolution fusion | flops 274203136 | bytes 5251072 | tf_op jit(solution)/shard_map/sub | solution.py:294
  71.9 3.8 fusion.22
  75.7 2.5 copy.198
  96.6 3.6 collective-permute-done.7
  103.0 14.1 %collective-permute-done.13 = bf16[256,1536]{1,0:T(8,128)(2,1)S(1)} collective-permute-done((bf16[256,1536]{1,0:T(8,128)(2,1)S(1)}, bf16[256,1536]{1,0:T(8,128)(2,1)S(1)}, u32[]{:S(2)}, u32[]{:S(2)}) %collective-permute-start.13) | collective-permute-done | bytes 786464 | tf_op jit(solution)/shard_map/ppermute | solution.py:36
  118.4 3.7 collective-permute-done.9
  128.1 3.1 fusion.133
  135.9 6.1 %shard_map.282 = (bf16[8,288,128]{2,1,0:T(8,128)(2,1)S(1)}, bf16[8,288,128]{2,1,0:T(8,128)(2,1)S(1)}, bf16[8,288,128]{2,1,0:T(8,128)(2,1)S(1)}, bf16[8,288,128]{...) custom-call(s32[3]{0:T(128)S(1)} %pad_add_fusion.coords, ...), custom_call_target="tpu_custom_call" | custom-call | flops 2415919104 | bytes 4718592 | tf_op jit(solution)/shard_map/pallas_call | solution.py:89
  142.0 3.1 collective-permute-start.81
  145.2 2.8 collective-permute-start.73
  152.1 6.6 %collective-permute-done.81 = bf16[8,288,128]{2,1,0:T(8,128)(2,1)S(1)} collective-permute-done((bf16[8,288,128]{2,1,0:T(8,128)(2,1)S(1)}, bf16[8,288,128]{2,1,0:T(8,128)(2,1)S(1)}, u32[]{:S(2)}, u32[]{:S(2)}) %collective-permute-start.81) | collective-permute-done | bytes 589856 | tf_op jit(solution)/shard_map/ppermute | solution.py:32
  169.5 2.7 collective-permute-start.83
  180.1 2.5 collective-permute-start.80
  214.8 2.4 copy.207
  236.2 2.6 collective-permute-done.26
  241.2 2.6 collective-permute-done.27
  244.3 3.8 shard_map.280
  252.1 3.4 collective-permute-done.29
  255.5 3.0 collective-permute-start.30
  261.2 3.1 collective-permute-done.89
  274.0 3.5 reshape.643
  277.5 4.3 copy.181
  281.8 4.6 %reshape.644 = f32[16384]{0:T(1024)} reshape(f32[1024,4,4]{2,1,0:T(4,128)} %copy.181) | data formatting | bytes 131072 | tf_op jit(solution)/shard_map/reshape | solution.py:364
  299.4 4.9 %collective-permute-done.45 = bf16[8,192,128]{2,1,0:T(8,128)(2,1)S(1)} collective-permute-done((bf16[8,192,128]{2,1,0:T(8,128)(2,1)S(1)}, bf16[8,192,128]{2,1,0:T(8,128)(2,1)S(1)}, u32[]{:S(2)}, u32[]{:S(2)}) %collective-permute-start.45) | collective-permute-done | bytes 393248 | tf_op jit(solution)/shard_map/ppermute | solution.py:32
  311.6 8.1 %collective-permute-done.46 = bf16[4,192,128]{2,1,0:T(8,128)(2,1)S(1)} collective-permute-done((bf16[4,192,128]{2,1,0:T(8,128)(2,1)S(1)}, bf16[4,192,128]{2,1,0:T(8,128)(2,1)S(1)}, u32[]{:S(2)}, u32[]{:S(2)}) %collective-permute-start.46) | collective-permute-done | bytes 196640 | tf_op jit(solution)/shard_map/ppermute | solution.py:32
  321.0 5.6 %collective-permute-done.42 = bf16[4,192,128]{2,1,0:T(8,128)(2,1)S(1)} collective-permute-done((bf16[4,192,128]{2,1,0:T(8,128)(2,1)S(1)}, bf16[4,192,128]{2,1,0:T(8,128)(2,1)S(1)}, u32[]{:S(2)}, u32[]{:S(2)}) %collective-permute-start.42) | collective-permute-done | bytes 196640 | tf_op jit(solution)/shard_map/ppermute | solution.py:32
  328.3 3.9 collective-permute-done.38
  333.2 7.0 %collective-permute-done.34 = bf16[4,192,128]{2,1,0:T(8,128)(2,1)S(1)} collective-permute-done((bf16[4,192,128]{2,1,0:T(8,128)(2,1)S(1)}, bf16[4,192,128]{2,1,0:T(8,128)(2,1)S(1)}, u32[]{:S(2)}, u32[]{:S(2)}) %collective-permute-start.34) | collective-permute-done | bytes 196640 | tf_op jit(solution)/shard_map/ppermute | solution.py:32
  344.8 2.8 collective-permute-start.39
  354.8 5.0 %collective-permute-done.48 = bf16[1,192,128]{2,1,0:T(8,128)(2,1)S(1)} collective-permute-done((bf16[1,192,128]{2,1,0:T(8,128)(2,1)S(1)}, bf16[1,192,128]{2,1,0:T(8,128)(2,1)S(1)}, u32[]{:S(2)}, u32[]{:S(2)}) %collective-permute-start.48) | collective-permute-done | bytes 49184 | tf_op jit(solution)/shard_map/ppermute | solution.py:32
  364.0 2.6 collective-permute-done.36
  372.9 3.7 collective-permute-done.51
  381.1 2.4 collective-permute-done.53
  385.3 8.0 %collective-permute-done.56 = bf16[1,192,128]{2,1,0:T(8,128)(2,1)S(1)} collective-permute-done((bf16[1,192,128]{2,1,0:T(8,128)(2,1)S(1)}, bf16[1,192,128]{2,1,0:T(8,128)(2,1)S(1)}, u32[]{:S(2)}, u32[]{:S(2)}) %collective-permute-start.56) | collective-permute-done | bytes 49184 | tf_op jit(solution)/shard_map/ppermute | solution.py:32
  400.8 2.5 collective-permute-done.57
  403.3 2.4 collective-permute-start.55
  406.7 4.9 %collective-permute-done.63 = bf16[2,192,128]{2,1,0:T(8,128)(2,1)S(1)} collective-permute-done((bf16[2,192,128]{2,1,0:T(8,128)(2,1)S(1)}, bf16[2,192,128]{2,1,0:T(8,128)(2,1)S(1)}, u32[]{:S(2)}, u32[]{:S(2)}) %collective-permute-start.63) | collective-permute-done | bytes 98336 | tf_op jit(solution)/shard_map/ppermute | solution.py:32
  413.3 4.0 collective-permute-done.58
  418.6 5.6 %collective-permute-done.64 = bf16[4,192,128]{2,1,0:T(8,128)(2,1)S(1)} collective-permute-done((bf16[4,192,128]{2,1,0:T(8,128)(2,1)S(1)}, bf16[4,192,128]{2,1,0:T(8,128)(2,1)S(1)}, u32[]{:S(2)}, u32[]{:S(2)}) %collective-permute-start.64) | collective-permute-done | bytes 196640 | tf_op jit(solution)/shard_map/ppermute | solution.py:32
  425.8 3.4 collective-permute-start.65
  429.2 2.5 collective-permute-start.66
  437.9 5.4 %shard_map.283 = (f32[256,3072]{1,0:T(8,128)}, f32[256,3072]{1,0:T(8,128)}, f32[768,1024]{1,0:T(8,128)}) custom-call(s32[3]{0:T(128)S(1)} %pad_add_fusion.coords, bf16[8,288,128]{2,1,0:T(8,128)(2,1)S(1)} %pad_maximum_fusion.12.refs_0_, bf16[8,288,128]{2,1,0:T(8,128)(2,1)S(1)} %pad_maximum_fusion.13.refs_1_, ...), custom_call_target="tpu_custom_call" | custom-call | bytes 14155776 | tf_op jit(solution)/shard_map/pallas_call | solution.py:141
  443.3 4.0 shard_map.281
  (689 shorter events, 237.8 us)
Async XLA Ops:
  0.7 25.4 %collective-permute-start.1 = (bf16[128,1024]{1,0:T(8,128)(2,1)}, bf16[128,1024]{1,0:T(8,128)(2,1)S(1)}, u32[]{:S(2)}, u32[]{:S(2)}) collective-permute-start(bf16[128,1024]{1,0:T(8,128)(2,1)} %param.19), channel_id=1, source_target_pairs={{0,2},{2,0},{1,3},{3,1},{4,6},{6,4},{5,7},{7,5},{8,10},{10,8},{9,1... | collective-permute-start | bytes 786440 | tf_op jit(solution)/shard_map/ppermute | solution.py:32
  2.7 31.0 %collective-permute-start = (bf16[128,1024]{1,0:T(8,128)(2,1)}, bf16[128,1024]{1,0:T(8,128)(2,1)S(1)}, u32[]{:S(2)}, u32[]{:S(2)}) collective-permute-start(bf16[128,1024]{1,0:T(8,128)(2,1)} %param.19), channel_id=1, source_target_pairs={{0,1},{1,0},{2,3},{3,2},{4,5},{5,4},{6,7},{7,6},{8,9},{9,8},{10,11... | collective-permute-start | bytes 786440 | tf_op jit(solution)/shard_map/ppermute | solution.py:32
  2.7 80.8 %collective-permute-start.17 = (bf16[128,1024]{1,0:T(8,128)(2,1)}, bf16[128,1024]{1,0:T(8,128)(2,1)}, u32[]{:S(2)}, u32[]{:S(2)}) collective-permute-start(bf16[128,1024]{1,0:T(8,128)(2,1)} %param.20), channel_id=1, source_target_pairs={{0,2},{2,0},{1,3},{3,1},{4,6},{6,4},{5,7},{7,5},{8,10},{10,8},{9,1... | collective-permute-start | bytes 786440 | tf_op jit(solution)/shard_map/ppermute | solution.py:32
  2.9 81.2 %collective-permute-start.16 = (bf16[128,1024]{1,0:T(8,128)(2,1)}, bf16[128,1024]{1,0:T(8,128)(2,1)}, u32[]{:S(2)}, u32[]{:S(2)}) collective-permute-start(bf16[128,1024]{1,0:T(8,128)(2,1)} %param.20), channel_id=1, source_target_pairs={{0,1},{1,0},{2,3},{3,2},{4,5},{5,4},{6,7},{7,6},{8,9},{9,8},{10,11... | collective-permute-start | bytes 786440 | tf_op jit(solution)/shard_map/ppermute | solution.py:32
  7.4 28.3 %collective-permute-start.3 = (bf16[2,256,1024]{2,1,0:T(8,128)(2,1)}, bf16[2,256,1024]{2,1,0:T(8,128)(2,1)}, u32[]{:S(2)}, u32[]{:S(2)}) collective-permute-start(bf16[2,256,1024]{2,1,0:T(8,128)(2,1)} %maximum_maximum_fusion.1), channel_id=1, source_target_pairs={{0,1},{1,0},{2,3},{3,2},{4,5},{5,4},{6,7},{7,6},{8,9},{9,8},{10,11... | collective-permute-start | bytes 3145736 | tf_op jit(solution)/shard_map/ppermute | solution.py:32
  33.7 16.4 %collective-permute-start.4 = (bf16[256,1024]{1,0:T(8,128)(2,1)}, bf16[256,1024]{1,0:T(8,128)(2,1)}, u32[]{:S(2)}, u32[]{:S(2)}) collective-permute-start(bf16[256,1024]{1,0:T(8,128)(2,1)} %pad_maximum_fusion.18), channel_id=1, source_target_pairs={{0,2},{2,64},{64,66},{66,0},{1,3},{3,65},{65,67},{67,1},{4,6},{6,6... | collective-permute-start | bytes 1572872 | tf_op jit(solution)/shard_map/ppermute | solution.py:36
  35.5 57.3 %collective-permute-start.11 = (bf16[2,256,1536]{2,1,0:T(8,128)(2,1)}, bf16[2,256,1536]{2,1,0:T(8,128)(2,1)}, u32[]{:S(2)}, u32[]{:S(2)}) collective-permute-start(bf16[2,256,1536]{2,1,0:T(8,128)(2,1)} %maximum_maximum_fusion), channel_id=1, source_target_pairs={{0,1},{1,0},{2,3},{3,2},{4,5},{5,4},{6,7},{7,6},{8,9},{9,8},{10,11... | collective-permute-start | bytes 4718600 | tf_op jit(solution)/shard_map/ppermute | solution.py:32
  37.9 14.8 %collective-permute-start.5 = (bf16[256,1024]{1,0:T(8,128)(2,1)}, bf16[256,1024]{1,0:T(8,128)(2,1)}, u32[]{:S(2)}, u32[]{:S(2)}) collective-permute-start(bf16[256,1024]{1,0:T(8,128)(2,1)} %get-tuple-element.210), channel_id=1, source_target_pairs={{0,66},{2,0},{64,2},{66,64},{1,67},{3,1},{65,3},{67,65},{4,70},{6,... | collective-permute-start | bytes 1572872 | tf_op jit(solution)/shard_map/ppermute | solution.py:36
  50.2 52.8 %collective-permute-start.12 = (bf16[256,1536]{1,0:T(8,128)(2,1)}, bf16[256,1536]{1,0:T(8,128)(2,1)}, u32[]{:S(2)}, u32[]{:S(2)}) collective-permute-start(bf16[256,1536]{1,0:T(8,128)(2,1)} %pad_maximum_fusion.11), channel_id=1, source_target_pairs={{0,2},{2,64},{64,66},{66,0},{1,3},{3,65},{65,67},{67,1},{4,6},{6,6... | collective-permute-start | bytes 2359304 | tf_op jit(solution)/shard_map/ppermute | solution.py:36
  94.3 22.7 %collective-permute-start.13 = (bf16[256,1536]{1,0:T(8,128)(2,1)S(1)}, bf16[256,1536]{1,0:T(8,128)(2,1)S(1)}, u32[]{:S(2)}, u32[]{:S(2)}) collective-permute-start(bf16[256,1536]{1,0:T(8,128)(2,1)S(1)} %get-tuple-element.180), channel_id=1, source_target_pairs={{0,66},{2,0},{64,2},{66,64},{1,67},{3,1},{65,3},{67,65},{4,70},{6,... | collective-permute-start | bytes 2359304 | tf_op jit(solution)/shard_map/ppermute | solution.py:36
  101.6 20.5 %collective-permute-start.9 = (bf16[128,1024]{1,0:T(8,128)(2,1)S(1)}, bf16[128,1024]{1,0:T(8,128)(2,1)S(1)}, u32[]{:S(2)}, u32[]{:S(2)}) collective-permute-start(bf16[128,1024]{1,0:T(8,128)(2,1)S(1)} %multiply_convert_fusion.6), channel_id=1, source_target_pairs={{0,2},{2,0},{1,3},{3,1},{4,6},{6,4},{5,7},{7,5},{8,10},{10,8},{9,1... | collective-permute-start | bytes 786440 | tf_op jit(solution)/shard_map/ppermute | solution.py:32
  102.9 19.6 %collective-permute-start.8 = (bf16[128,1024]{1,0:T(8,128)(2,1)S(1)}, bf16[128,1024]{1,0:T(8,128)(2,1)S(1)}, u32[]{:S(2)}, u32[]{:S(2)}) collective-permute-start(bf16[128,1024]{1,0:T(8,128)(2,1)S(1)} %multiply_convert_fusion.6), channel_id=1, source_target_pairs={{0,1},{1,0},{2,3},{3,2},{4,5},{5,4},{6,7},{7,6},{8,9},{9,8},{10,11... | collective-permute-start | bytes 786440 | tf_op jit(solution)/shard_map/ppermute | solution.py:32
  132.1 15.8 %collective-permute-start.19 = (bf16[2,128,1024]{2,1,0:T(8,128)(2,1)}, bf16[2,128,1024]{2,1,0:T(8,128)(2,1)}, u32[]{:S(2)}, u32[]{:S(2)}) collective-permute-start(bf16[2,128,1024]{2,1,0:T(8,128)(2,1)} %pad_maximum_fusion.22), channel_id=1, source_target_pairs={{0,1},{1,0},{2,3},{3,2},{4,5},{5,4},{6,7},{7,6},{8,9},{9,8},{10,11... | collective-permute-start | bytes 1572872 | tf_op jit(solution)/shard_map/ppermute | solution.py:32
  134.2 16.2 %collective-permute-start.14 = (bf16[2,128,1024]{2,1,0:T(8,128)(2,1)}, bf16[2,128,1024]{2,1,0:T(8,128)(2,1)S(1)}, u32[]{:S(2)}, u32[]{:S(2)}) collective-permute-start(bf16[2,128,1024]{2,1,0:T(8,128)(2,1)} %pad_maximum_fusion.21), channel_id=1, source_target_pairs={{0,1},{1,0},{2,3},{3,2},{4,5},{5,4},{6,7},{7,6},{8,9},{9,8},{10,11... | collective-permute-start | bytes 1572872 | tf_op jit(solution)/shard_map/ppermute | solution.py:32
  142.0 16.7 %collective-permute-start.81 = (bf16[8,288,128]{2,1,0:T(8,128)(2,1)S(1)}, bf16[8,288,128]{2,1,0:T(8,128)(2,1)S(1)}, u32[]{:S(2)}, u32[]{:S(2)}) collective-permute-start(bf16[8,288,128]{2,1,0:T(8,128)(2,1)S(1)} %get-tuple-element.58), channel_id=1, source_target_pairs={{0,48},{16,32},{32,16},{48,0},{1,49},{17,33},{33,17},{49,1},{2,50}... | collective-permute-start | bytes 1769480 | tf_op jit(solution)/shard_map/ppermute | solution.py:32
  145.0 15.1 %collective-permute-start.77 = (bf16[8,288,128]{2,1,0:T(8,128)(2,1)S(1)}, bf16[8,288,128]{2,1,0:T(8,128)(2,1)S(1)}, u32[]{:S(2)}, u32[]{:S(2)}) collective-permute-start(bf16[8,288,128]{2,1,0:T(8,128)(2,1)S(1)} %get-tuple-element.56), channel_id=1, source_target_pairs={{0,16},{16,0},{32,48},{48,32},{1,17},{17,1},{33,49},{49,33},{2,18}... | collective-permute-start | bytes 1769480 | tf_op jit(solution)/shard_map/ppermute | solution.py:32
  145.2 17.0 %collective-permute-start.73 = (bf16[8,288,128]{2,1,0:T(8,128)(2,1)S(1)}, bf16[8,288,128]{2,1,0:T(8,128)(2,1)S(1)}, u32[]{:S(2)}, u32[]{:S(2)}) collective-permute-start(bf16[8,288,128]{2,1,0:T(8,128)(2,1)S(1)} %get-tuple-element.54), channel_id=1, source_target_pairs={{0,12},{4,8},{8,4},{12,0},{1,13},{5,9},{9,5},{13,1},{2,14},{6,10},... | collective-permute-start | bytes 1769480 | tf_op jit(solution)/shard_map/ppermute | solution.py:32
  148.0 16.2 %collective-permute-start.69 = (bf16[8,288,128]{2,1,0:T(8,128)(2,1)S(1)}, bf16[8,288,128]{2,1,0:T(8,128)(2,1)S(1)}, u32[]{:S(2)}, u32[]{:S(2)}) collective-permute-start(bf16[8,288,128]{2,1,0:T(8,128)(2,1)S(1)} %get-tuple-element.52), channel_id=1, source_target_pairs={{0,4},{4,0},{8,12},{12,8},{1,5},{5,1},{9,13},{13,9},{2,6},{6,2},{1... | collective-permute-start | bytes 1769480 | tf_op jit(solution)/shard_map/ppermute | solution.py:32
  150.5 16.1 %collective-permute-start.20 = (bf16[128,1024]{1,0:T(8,128)(2,1)S(1)}, bf16[128,1024]{1,0:T(8,128)(2,1)S(1)}, u32[]{:S(2)}, u32[]{:S(2)}) collective-permute-start(bf16[128,1024]{1,0:T(8,128)(2,1)S(1)} %fusion.48), channel_id=1, source_target_pairs={{0,2},{2,0},{1,3},{3,1},{4,6},{6,4},{5,7},{7,5},{8,10},{10,8},{9,1... | collective-permute-start | bytes 786440 | tf_op jit(solution)/shard_map/ppermute | solution.py:32
  168.2 15.1 %collective-permute-start.22 = (bf16[128,1024]{1,0:T(8,128)(2,1)S(1)}, bf16[128,1024]{1,0:T(8,128)(2,1)S(1)}, u32[]{:S(2)}, u32[]{:S(2)}) collective-permute-start(bf16[128,1024]{1,0:T(8,128)(2,1)S(1)} %fusion.114), channel_id=1, source_target_pairs={{0,2},{2,0},{1,3},{3,1},{4,6},{6,4},{5,7},{7,5},{8,10},{10,8},{9,1... | collective-permute-start | bytes 786440 | tf_op jit(solution)/shard_map/ppermute | solution.py:32
  168.3 29.5 %collective-permute-start.21 = (bf16[128,1024]{1,0:T(8,128)(2,1)S(1)}, bf16[128,1024]{1,0:T(8,128)(2,1)S(1)}, u32[]{:S(2)}, u32[]{:S(2)}) collective-permute-start(bf16[128,1024]{1,0:T(8,128)(2,1)S(1)} %fusion.114), channel_id=1, source_target_pairs={{0,1},{1,0},{2,3},{3,2},{4,5},{5,4},{6,7},{7,6},{8,9},{9,8},{10,11... | collective-permute-start | bytes 786440 | tf_op jit(solution)/shard_map/ppermute | solution.py:32
  183.8 14.0 %collective-permute-start.23 = (bf16[128,1024]{1,0:T(8,128)(2,1)S(1)}, bf16[128,1024]{1,0:T(8,128)(2,1)S(1)}, u32[]{:S(2)}, u32[]{:S(2)}) collective-permute-start(bf16[128,1024]{1,0:T(8,128)(2,1)S(1)} %collective-permute-done.22), channel_id=1, source_target_pairs={{0,1},{1,0},{2,3},{3,2},{4,5},{5,4},{6,7},{7,6},{8,9},{9,8},{10,11... | collective-permute-start | bytes 786440 | tf_op jit(solution)/shard_map/ppermute | solution.py:32
  194.8 56.2 %collective-permute-start.86 = (bf16[4,192,128]{2,1,0:T(8,128)(2,1)}, bf16[4,192,128]{2,1,0:T(8,128)(2,1)}, u32[]{:S(2)}, u32[]{:S(2)}) collective-permute-start(bf16[4,192,128]{2,1,0:T(8,128)(2,1)} %fusion.89), channel_id=1, source_target_pairs={{0,64},{64,0},{1,65},{65,1},{2,66},{66,2},{3,67},{67,3},{4,68},{68... | collective-permute-start | bytes 589832 | tf_op jit(solution)/shard_map/ppermute | solution.py:32
  241.2 68.8 %collective-permute-start.24 = (bf16[2,128,1024]{2,1,0:T(8,128)(2,1)}, bf16[2,128,1024]{2,1,0:T(8,128)(2,1)}, u32[]{:S(2)}, u32[]{:S(2)}) collective-permute-start(bf16[2,128,1024]{2,1,0:T(8,128)(2,1)} %pad_maximum_fusion.24), channel_id=1, source_target_pairs={{0,1},{1,0},{2,3},{3,2},{4,5},{5,4},{6,7},{7,6},{8,9},{9,8},{10,11... | collective-permute-start | bytes 1572872 | tf_op jit(solution)/shard_map/ppermute | solution.py:32
  265.9 26.3 %collective-permute-start.90 = (bf16[2,288,128]{2,1,0:T(8,128)(2,1)}, bf16[2,288,128]{2,1,0:T(8,128)(2,1)}, u32[]{:S(2)}, u32[]{:S(2)}) collective-permute-start(bf16[2,288,128]{2,1,0:T(8,128)(2,1)} %pad_maximum_fusion.43), channel_id=1, source_target_pairs={{0,16},{16,0},{32,48},{48,32},{1,17},{17,1},{33,49},{49,33},{2,18}... | collective-permute-start | bytes 442376 | tf_op jit(solution)/shard_map/ppermute | solution.py:32
  266.6 26.4 %collective-permute-start.93 = (bf16[2,288,128]{2,1,0:T(8,128)(2,1)}, bf16[2,288,128]{2,1,0:T(8,128)(2,1)}, u32[]{:S(2)}, u32[]{:S(2)}) collective-permute-start(bf16[2,288,128]{2,1,0:T(8,128)(2,1)} %pad_maximum_fusion.44), channel_id=1, source_target_pairs={{0,48},{16,32},{32,16},{48,0},{1,49},{17,33},{33,17},{49,1},{2,50}... | collective-permute-start | bytes 442376 | tf_op jit(solution)/shard_map/ppermute | solution.py:32
  269.1 24.3 %collective-permute-start.96 = (bf16[2,288,128]{2,1,0:T(8,128)(2,1)}, bf16[2,288,128]{2,1,0:T(8,128)(2,1)}, u32[]{:S(2)}, u32[]{:S(2)}) collective-permute-start(bf16[2,288,128]{2,1,0:T(8,128)(2,1)} %pad_maximum_fusion.45), channel_id=1, source_target_pairs={{0,4},{4,0},{8,12},{12,8},{1,5},{5,1},{9,13},{13,9},{2,6},{6,2},{1... | collective-permute-start | bytes 442376 | tf_op jit(solution)/shard_map/ppermute | solution.py:32
  271.7 23.7 %collective-permute-start.99 = (bf16[2,288,128]{2,1,0:T(8,128)(2,1)}, bf16[2,288,128]{2,1,0:T(8,128)(2,1)}, u32[]{:S(2)}, u32[]{:S(2)}) collective-permute-start(bf16[2,288,128]{2,1,0:T(8,128)(2,1)} %pad_maximum_fusion.46), channel_id=1, source_target_pairs={{0,12},{4,8},{8,4},{12,0},{1,13},{5,9},{9,5},{13,1},{2,14},{6,10},... | collective-permute-start | bytes 442376 | tf_op jit(solution)/shard_map/ppermute | solution.py:32
  292.2 12.1 %collective-permute-start.45 = (bf16[8,192,128]{2,1,0:T(8,128)(2,1)S(1)}, bf16[8,192,128]{2,1,0:T(8,128)(2,1)S(1)}, u32[]{:S(2)}, u32[]{:S(2)}) collective-permute-start(bf16[8,192,128]{2,1,0:T(8,128)(2,1)S(1)} %copy-done.7), channel_id=1, source_target_pairs={{0,48},{16,32},{32,16},{48,0},{1,49},{17,33},{33,17},{49,1},{2,50}... | collective-permute-start | bytes 1179656 | tf_op jit(solution)/shard_map/ppermute | solution.py:32
  293.0 12.6 %collective-permute-start.41 = (bf16[8,192,128]{2,1,0:T(8,128)(2,1)S(1)}, bf16[8,192,128]{2,1,0:T(8,128)(2,1)S(1)}, u32[]{:S(2)}, u32[]{:S(2)}) collective-permute-start(bf16[8,192,128]{2,1,0:T(8,128)(2,1)S(1)} %copy-done.5), channel_id=1, source_target_pairs={{0,16},{16,0},{32,48},{48,32},{1,17},{17,1},{33,49},{49,33},{2,18}... | collective-permute-start | bytes 1179656 | tf_op jit(solution)/shard_map/ppermute | solution.py:32
  293.4 12.4 %collective-permute-start.37 = (bf16[8,192,128]{2,1,0:T(8,128)(2,1)S(1)}, bf16[8,192,128]{2,1,0:T(8,128)(2,1)S(1)}, u32[]{:S(2)}, u32[]{:S(2)}) collective-permute-start(bf16[8,192,128]{2,1,0:T(8,128)(2,1)S(1)} %copy-done.3), channel_id=1, source_target_pairs={{0,12},{4,8},{8,4},{12,0},{1,13},{5,9},{9,5},{13,1},{2,14},{6,10},... | collective-permute-start | bytes 1179656 | tf_op jit(solution)/shard_map/ppermute | solution.py:32
  295.4 12.6 %collective-permute-start.33 = (bf16[8,192,128]{2,1,0:T(8,128)(2,1)S(1)}, bf16[8,192,128]{2,1,0:T(8,128)(2,1)S(1)}, u32[]{:S(2)}, u32[]{:S(2)}) collective-permute-start(bf16[8,192,128]{2,1,0:T(8,128)(2,1)S(1)} %get-tuple-element.40), channel_id=1, source_target_pairs={{0,4},{4,0},{8,12},{12,8},{1,5},{5,1},{9,13},{13,9},{2,6},{6,2},{1... | collective-permute-start | bytes 1179656 | tf_op jit(solution)/shard_map/ppermute | solution.py:32
  304.3 36.9 %collective-permute-start.91 = (bf16[4,288,128]{2,1,0:T(8,128)(2,1)S(1)}, bf16[4,288,128]{2,1,0:T(8,128)(2,1)S(1)}, u32[]{:S(2)}, u32[]{:S(2)}) collective-permute-start(bf16[4,288,128]{2,1,0:T(8,128)(2,1)S(1)} %pad_maximum_fusion.33), channel_id=1, source_target_pairs={{0,12},{4,8},{8,4},{12,0},{1,13},{5,9},{9,5},{13,1},{2,14},{6,10},... | collective-permute-start | bytes 884744 | tf_op jit(solution)/shard_map/ppermute | solution.py:32
  305.6 38.1 %collective-permute-start.94 = (bf16[4,288,128]{2,1,0:T(8,128)(2,1)S(1)}, bf16[4,288,128]{2,1,0:T(8,128)(2,1)S(1)}, u32[]{:S(2)}, u32[]{:S(2)}) collective-permute-start(bf16[4,288,128]{2,1,0:T(8,128)(2,1)S(1)} %pad_maximum_fusion.34), channel_id=1, source_target_pairs={{0,4},{4,0},{8,12},{12,8},{1,5},{5,1},{9,13},{13,9},{2,6},{6,2},{1... | collective-permute-start | bytes 884744 | tf_op jit(solution)/shard_map/ppermute | solution.py:32
  305.8 38.9 %collective-permute-start.97 = (bf16[4,288,128]{2,1,0:T(8,128)(2,1)S(1)}, bf16[4,288,128]{2,1,0:T(8,128)(2,1)S(1)}, u32[]{:S(2)}, u32[]{:S(2)}) collective-permute-start(bf16[4,288,128]{2,1,0:T(8,128)(2,1)S(1)} %pad_maximum_fusion.35), channel_id=1, source_target_pairs={{0,48},{16,32},{32,16},{48,0},{1,49},{17,33},{33,17},{49,1},{2,50}... | collective-permute-start | bytes 884744 | tf_op jit(solution)/shard_map/ppermute | solution.py:32
  308.0 62.0 %collective-permute-start.100 = (bf16[4,288,128]{2,1,0:T(8,128)(2,1)S(1)}, bf16[4,288,128]{2,1,0:T(8,128)(2,1)S(1)}, u32[]{:S(2)}, u32[]{:S(2)}) collective-permute-start(bf16[4,288,128]{2,1,0:T(8,128)(2,1)S(1)} %pad_maximum_fusion.36), channel_id=1, source_target_pairs={{0,16},{16,0},{32,48},{48,32},{1,17},{17,1},{33,49},{49,33},{2,18}... | collective-permute-start | bytes 884744 | tf_op jit(solution)/shard_map/ppermute | solution.py:32
  340.2 39.5 %collective-permute-start.25 = (bf16[128,1024]{1,0:T(8,128)(2,1)S(1)}, bf16[128,1024]{1,0:T(8,128)(2,1)S(1)}, u32[]{:S(2)}, u32[]{:S(2)}) collective-permute-start(bf16[128,1024]{1,0:T(8,128)(2,1)S(1)} %fusion.43), channel_id=1, source_target_pairs={{0,2},{2,0},{1,3},{3,1},{4,6},{6,4},{5,7},{7,5},{8,10},{10,8},{9,1... | collective-permute-start | bytes 786440 | tf_op jit(solution)/shard_map/ppermute | solution.py:32
  349.5 79.7 %collective-permute-start.101 = (bf16[8,288,128]{2,1,0:T(8,128)(2,1)S(1)}, bf16[8,288,128]{2,1,0:T(8,128)(2,1)S(1)}, u32[]{:S(2)}, u32[]{:S(2)}) collective-permute-start(bf16[8,288,128]{2,1,0:T(8,128)(2,1)S(1)} %pad_maximum_fusion.12.refs_0_), channel_id=1, source_target_pairs={{0,4},{4,0},{8,12},{12,8},{1,5},{5,1},{9,13},{13,9},{2,6},{6,2},{1... | collective-permute-start | bytes 1769480 | tf_op jit(solution)/shard_map/ppermute | solution.py:32
  368.0 10.0 %collective-permute-start.50 = (bf16[4,128,128]{2,1,0:T(8,128)(2,1)S(1)}, bf16[4,128,128]{2,1,0:T(8,128)(2,1)S(1)}, u32[]{:S(2)}, u32[]{:S(2)}) collective-permute-start(bf16[4,128,128]{2,1,0:T(8,128)(2,1)S(1)} %fusion.100), channel_id=1, source_target_pairs={{0,64},{64,0},{1,65},{65,1},{2,66},{66,2},{3,67},{67,3},{4,68},{68... | collective-permute-start | bytes 393224 | tf_op jit(solution)/shard_map/ppermute | solution.py:32
  376.5 55.2 %collective-permute-start.102 = (bf16[8,288,128]{2,1,0:T(8,128)(2,1)S(1)}, bf16[8,288,128]{2,1,0:T(8,128)(2,1)S(1)}, u32[]{:S(2)}, u32[]{:S(2)}) collective-permute-start(bf16[8,288,128]{2,1,0:T(8,128)(2,1)S(1)} %pad_maximum_fusion.13.refs_1_), channel_id=1, source_target_pairs={{0,12},{4,8},{8,4},{12,0},{1,13},{5,9},{9,5},{13,1},{2,14},{6,10},... | collective-permute-start | bytes 1769480 | tf_op jit(solution)/shard_map/ppermute | solution.py:32
  377.4 54.3 %collective-permute-start.103 = (bf16[8,288,128]{2,1,0:T(8,128)(2,1)S(1)}, bf16[8,288,128]{2,1,0:T(8,128)(2,1)S(1)}, u32[]{:S(2)}, u32[]{:S(2)}) collective-permute-start(bf16[8,288,128]{2,1,0:T(8,128)(2,1)S(1)} %pad_maximum_fusion.14.refs_2_), channel_id=1, source_target_pairs={{0,16},{16,0},{32,48},{48,32},{1,17},{17,1},{33,49},{49,33},{2,18}... | collective-permute-start | bytes 1769480 | tf_op jit(solution)/shard_map/ppermute | solution.py:32
  379.9 13.5 %collective-permute-start.56 = (bf16[1,192,128]{2,1,0:T(8,128)(2,1)S(1)}, bf16[1,192,128]{2,1,0:T(8,128)(2,1)S(1)}, u32[]{:S(2)}, u32[]{:S(2)}) collective-permute-start(bf16[1,192,128]{2,1,0:T(8,128)(2,1)S(1)} %get-tuple-element.224), channel_id=1, source_target_pairs={{0,16},{16,0},{32,48},{48,32},{1,17},{17,1},{33,49},{49,33},{2,18}... | collective-permute-start | bytes 147464 | tf_op jit(solution)/shard_map/ppermute | solution.py:32
  383.5 11.3 %collective-permute-start.59 = (bf16[1,192,128]{2,1,0:T(8,128)(2,1)S(1)}, bf16[1,192,128]{2,1,0:T(8,128)(2,1)S(1)}, u32[]{:S(2)}, u32[]{:S(2)}) collective-permute-start(bf16[1,192,128]{2,1,0:T(8,128)(2,1)S(1)} %get-tuple-element.223), channel_id=1, source_target_pairs={{0,12},{4,8},{8,4},{12,0},{1,13},{5,9},{9,5},{13,1},{2,14},{6,10},... | collective-permute-start | bytes 147464 | tf_op jit(solution)/shard_map/ppermute | solution.py:32
  424.2 13.7 %collective-permute-start.104 = (bf16[8,288,128]{2,1,0:T(8,128)(2,1)S(1)}, bf16[8,288,128]{2,1,0:T(8,128)(2,1)S(1)}, u32[]{:S(2)}, u32[]{:S(2)}) collective-permute-start(bf16[8,288,128]{2,1,0:T(8,128)(2,1)S(1)} %pad_maximum_fusion.15.refs_3_), channel_id=1, source_target_pairs={{0,48},{16,32},{32,16},{48,0},{1,49},{17,33},{33,17},{49,1},{2,50}... | collective-permute-start | bytes 1769480 | tf_op jit(solution)/shard_map/ppermute | solution.py:32
  425.8 17.5 %collective-permute-start.65 = (bf16[8,192,128]{2,1,0:T(8,128)(2,1)S(1)}, bf16[8,192,128]{2,1,0:T(8,128)(2,1)S(1)}, u32[]{:S(2)}, u32[]{:S(2)}) collective-permute-start(bf16[8,192,128]{2,1,0:T(8,128)(2,1)S(1)} %pad_maximum_fusion.25.refs_0_), channel_id=1, source_target_pairs={{0,4},{4,0},{8,12},{12,8},{1,5},{5,1},{9,13},{13,9},{2,6},{6,2},{1... | collective-permute-start | bytes 1179656 | tf_op jit(solution)/shard_map/ppermute | solution.py:32
  429.2 14.1 %collective-permute-start.66 = (bf16[8,192,128]{2,1,0:T(8,128)(2,1)S(1)}, bf16[8,192,128]{2,1,0:T(8,128)(2,1)S(1)}, u32[]{:S(2)}, u32[]{:S(2)}) collective-permute-start(bf16[8,192,128]{2,1,0:T(8,128)(2,1)S(1)} %pad_maximum_fusion.26.refs_1_), channel_id=1, source_target_pairs={{0,12},{4,8},{8,4},{12,0},{1,13},{5,9},{9,5},{13,1},{2,14},{6,10},... | collective-permute-start | bytes 1179656 | tf_op jit(solution)/shard_map/ppermute | solution.py:32
  431.7 11.6 %collective-permute-start.67 = (bf16[8,192,128]{2,1,0:T(8,128)(2,1)S(1)}, bf16[8,192,128]{2,1,0:T(8,128)(2,1)S(1)}, u32[]{:S(2)}, u32[]{:S(2)}) collective-permute-start(bf16[8,192,128]{2,1,0:T(8,128)(2,1)S(1)} %pad_maximum_fusion.27.refs_2_), channel_id=1, source_target_pairs={{0,16},{16,0},{32,48},{48,32},{1,17},{17,1},{33,49},{49,33},{2,18}... | collective-permute-start | bytes 1179656 | tf_op jit(solution)/shard_map/ppermute | solution.py:32
  431.7 11.6 %collective-permute-start.68 = (bf16[8,192,128]{2,1,0:T(8,128)(2,1)S(1)}, bf16[8,192,128]{2,1,0:T(8,128)(2,1)S(1)}, u32[]{:S(2)}, u32[]{:S(2)}) collective-permute-start(bf16[8,192,128]{2,1,0:T(8,128)(2,1)S(1)} %pad_maximum_fusion.28.refs_3_), channel_id=1, source_target_pairs={{0,48},{16,32},{32,16},{48,0},{1,49},{17,33},{33,17},{49,1},{2,50}... | collective-permute-start | bytes 1179656 | tf_op jit(solution)/shard_map/ppermute | solution.py:32
  (175 other events, 1650.7 us)
